TPU v7x, 512 devices: a whole 4x8x8 slice. The times are simulated.
512 devices in a mesh: visit: 128 (over z, x_hi, y), quad: 4 (over x_lo, core).
Axes of the slice: x: 4 (x_hi: 2, x_lo: 2; x = x_hi * 2 + x_lo), y: 8, z: 8, core: 2. Of those that a mesh axis runs over, the one named last changes fastest.
Arguments:
- science: float32 [256, 192, 1024], P('visit', 'quad'), may hold values from -80 to 80
- reference_tiles: float32 [256, 192, 1024], P('visit', 'quad'), may hold values from -20 to 20
- visit_tiles: int32 [256, 2], P('visit'), may hold values from 0 to 255, as said below
- offsets: int32 [256], P('visit'), may hold values from 1 to 1023
- basis_rows: float32 [31, 31], replicated, may hold values from -1 to 2
- basis_cols: float32 [31, 31], replicated, may hold values from -1 to 2
Outputs:
- difference: float32 [256, 192, 1024], P('visit', 'quad')
- coadd_tiles: float32 [256, 192, 1024], P('visit', 'quad')
Inputs may be any that keep to these rules, and one draw needn't show every extreme that they name: `visit_tiles`: tile t belongs to device t // 2 of visit and visit v to device v // 2; each of a visit's two tiles lies on a device at most 3 steps away, counted cyclically, and in every draw some visit's left tile is 3 steps ahead and some visit's right tile 3 steps behind. A visit's two tiles differ.
All inputs are finite; a program needn't handle non-finite values.
Results may differ from a plain program's by a relative error of at most 0.0003.
Values sent between devices are 32-bit elements; how exact they have to be, the bound alone decides.
A program may use at most 64 MiB of HBM per device.

v0:
```python
import jax
import jax.numpy as jnp
from jax import lax
from jax.sharding import PartitionSpec as P

REACH = 3


HIGHEST = lax.Precision.HIGHEST
BLOCK_COLS = 128


def passed_along(x, axis, by):
    count = lax.axis_size(axis)
    return lax.ppermute(x, axis, [(i, (i + by) % count) for i in range(count)])


def extended(block, sides, width):
    for axis, dim in sides:
        count = lax.axis_size(axis)
        forward = [(i, i + 1) for i in range(count - 1)]
        backward = [(target, source) for source, target in forward]
        low = lax.ppermute(
            lax.slice_in_dim(block, block.shape[dim] - width, None, axis=dim), axis, forward
        )
        high = lax.ppermute(lax.slice_in_dim(block, 0, width, axis=dim), axis, backward)
        block = jnp.concatenate([low, block, high], axis=dim)
    return block


def row_weights(basis_rows, local_rows):
    tap_count = basis_rows.shape[1]
    padded_rows = local_rows + tap_count - 1
    tap_index = lax.broadcasted_iota(jnp.int32, (tap_count, local_rows, padded_rows), 0)
    out_row = lax.broadcasted_iota(jnp.int32, (tap_count, local_rows, padded_rows), 1)
    source_row = lax.broadcasted_iota(jnp.int32, (tap_count, local_rows, padded_rows), 2)
    selector = (source_row - out_row == tap_index).astype(jnp.float32)
    return jnp.einsum("bt,tys->bys", basis_rows, selector, precision=HIGHEST)


def column_band(basis_cols):
    tap_count = basis_cols.shape[1]
    window = BLOCK_COLS + tap_count - 1
    tap_index = lax.broadcasted_iota(jnp.int32, (tap_count, window, BLOCK_COLS), 0)
    source_col = lax.broadcasted_iota(jnp.int32, (tap_count, window, BLOCK_COLS), 1)
    out_col = lax.broadcasted_iota(jnp.int32, (tap_count, window, BLOCK_COLS), 2)
    selector = (source_col - out_col == tap_index).astype(jnp.float32)
    return jnp.einsum("bt,twc->wbc", basis_cols, selector, precision=HIGHEST)


def on_device(science, reference_tiles, visit_tiles, offsets, basis_rows, basis_cols):
    visit_count = lax.axis_size("visit")
    own_index = lax.axis_index("visit")
    tap_count = basis_rows.shape[1]
    half_width = tap_count // 2
    basis_count = basis_rows.shape[0]
    visit_slots = science.shape[0]
    local_rows = science.shape[1]
    col_count = science.shape[2]
    per_device = reference_tiles.shape[0]
    block_count = col_count // BLOCK_COLS
    distances = [
        step_size * sign_value for step_size in range(1, REACH + 1) for sign_value in (1, -1)
    ]
    received = {0: reference_tiles}
    for distance in distances:
        received[-distance] = passed_along(reference_tiles, "visit", distance)
    tile_bank = jnp.concatenate([received[delta] for delta in range(-REACH, REACH + 1)], axis=0)

    def bank_slot(tile_id):
        owner = tile_id // per_device
        delta = (owner - own_index + REACH + visit_count) % visit_count - REACH
        return (delta + REACH) * per_device + tile_id % per_device

    templates = []
    for visit_slot in range(visit_slots):
        first_tile = lax.dynamic_index_in_dim(
            tile_bank, bank_slot(visit_tiles[visit_slot, 0]), 0, keepdims=False
        )
        second_tile = lax.dynamic_index_in_dim(
            tile_bank, bank_slot(visit_tiles[visit_slot, 1]), 0, keepdims=False
        )
        joined = jnp.concatenate([first_tile, second_tile], axis=1)
        templates.append(lax.dynamic_slice_in_dim(joined, offsets[visit_slot], col_count, 1))
    templates = jnp.stack(templates)
    templates = extended(templates, (("quad", 1),), half_width)
    padded = jnp.pad(templates, ((0, 0), (0, 0), (half_width, half_width)))
    window = BLOCK_COLS + tap_count - 1
    segments = jnp.stack(
        [
            padded[:, :, first_col : first_col + window]
            for first_col in range(0, col_count, BLOCK_COLS)
        ],
        axis=1,
    )
    band = column_band(basis_cols)
    weights = row_weights(basis_rows, local_rows)
    along_cols = jnp.einsum("vnsw,wbc->vnsbc", segments, band, precision=HIGHEST)
    images = jnp.einsum("bys,vnsbc->vnbyc", weights, along_cols, precision=HIGHEST)
    target = science.reshape(visit_slots, local_rows, block_count, BLOCK_COLS)
    normals = jnp.einsum("vnbyc,vnjyc->vbj", images, images, precision=HIGHEST)
    moments = jnp.einsum("vnbyc,vync->vb", images, target, precision=HIGHEST)
    normal_sum, moment_sum = lax.psum((normals, moments), "quad")
    pixels = lax.axis_size("quad") * local_rows * col_count
    solved = []
    for visit_slot in range(visit_slots):
        system = normal_sum[visit_slot] / pixels + 0.01 * jnp.eye(basis_count, dtype=jnp.float32)
        factor = jnp.linalg.cholesky(system)
        solved.append(jax.scipy.linalg.cho_solve((factor, True), moment_sum[visit_slot] / pixels))
    coefficients = jnp.stack(solved)
    matched = jnp.einsum("vb,vnbyc->vync", coefficients, images, precision=HIGHEST)
    difference = science - matched.reshape(visit_slots, local_rows, col_count)
    bank_size = (2 * REACH + 1) * per_device
    parts = []
    slot_ids = []
    for visit_slot in range(visit_slots):
        placed = lax.dynamic_update_slice(
            jnp.zeros((local_rows, 2 * col_count), jnp.float32),
            difference[visit_slot],
            (jnp.int32(0), offsets[visit_slot]),
        )
        parts.append(placed[:, :col_count])
        parts.append(placed[:, col_count:])
        slot_ids.append(bank_slot(visit_tiles[visit_slot, 0]))
        slot_ids.append(bank_slot(visit_tiles[visit_slot, 1]))
    selector = (
        jnp.stack(slot_ids)[:, None] == jnp.arange(bank_size, dtype=jnp.int32)[None, :]
    ).astype(jnp.float32)
    shares = jnp.einsum("pk,pyx->kyx", selector, jnp.stack(parts), precision=HIGHEST)
    shares = shares.reshape(2 * REACH + 1, per_device, local_rows, col_count)
    coadd_tiles = shares[REACH]
    for distance in distances:
        coadd_tiles = coadd_tiles + passed_along(shares[REACH + distance], "visit", distance)
    return (difference, coadd_tiles)


def solution(mesh):
    placed = (
        P("visit", "quad", None),
        P("visit", "quad", None),
        P("visit", None),
        P("visit"),
        P(),
        P(),
    )
    return jax.shard_map(
        on_device,
        mesh=mesh,
        in_specs=placed,
        out_specs=(P("visit", "quad", None), P("visit", "quad", None)),
        check_vma=False,
    )
```

profile of v0, /device:TPU:1, one launch (start us, length us, event | category | flops | bytes accessed | tf_op | source)
XLA Modules:
  0.0 317.6 jit_solution(7745542973765789139)
XLA Ops:
  0.7 6.2 %collective-permute-start = (f32[2,48,1024]{2,1,0:T(8,128)}, f32[2,48,1024]{2,1,0:T(8,128)}, u32[]{:S(2)}, u32[]{:S(2)}) collective-permute-start(f32[2,48,1024]{2,1,0:T(8,128)} %param.10), channel_id=1, source_target_pairs={{0,12},{4,16},{8,20},{12,24},{16,28},{20,32},{24,36},{28,40},{32,4... | collective-permute-start | bytes 1179656 | tf_op jit(solution)/shard_map/ppermute | solution.py:15
  6.9 4.5 %collective-permute-start.1 = (f32[2,48,1024]{2,1,0:T(8,128)}, f32[2,48,1024]{2,1,0:T(8,128)}, u32[]{:S(2)}, u32[]{:S(2)}) collective-permute-start(f32[2,48,1024]{2,1,0:T(8,128)} %param.10), channel_id=1, source_target_pairs={{0,8},{4,12},{8,16},{12,20},{16,24},{20,28},{24,32},{28,36},{32,40... | collective-permute-start | bytes 1179656 | tf_op jit(solution)/shard_map/ppermute | solution.py:15
  11.4 2.3 collective-permute-start.2
  13.7 9.7 %collective-permute-start.3 = (f32[2,48,1024]{2,1,0:T(8,128)}, f32[2,48,1024]{2,1,0:T(8,128)}, u32[]{:S(2)}, u32[]{:S(2)}) collective-permute-start(f32[2,48,1024]{2,1,0:T(8,128)} %param.10), channel_id=1, source_target_pairs={{0,508},{4,0},{8,4},{12,8},{16,12},{20,16},{24,20},{28,24},{32,28}... | collective-permute-start | bytes 1179656 | tf_op jit(solution)/shard_map/ppermute | solution.py:15
  23.5 4.3 %collective-permute-start.4 = (f32[2,48,1024]{2,1,0:T(8,128)}, f32[2,48,1024]{2,1,0:T(8,128)S(1)}, u32[]{:S(2)}, u32[]{:S(2)}) collective-permute-start(f32[2,48,1024]{2,1,0:T(8,128)} %param.10), channel_id=1, source_target_pairs={{0,504},{4,508},{8,0},{12,4},{16,8},{20,12},{24,16},{28,20},{32,24... | collective-permute-start | bytes 1179656 | tf_op jit(solution)/shard_map/ppermute | solution.py:15
  27.7 0.3 iota_compare_fusion
  28.0 1.3 fusion.6
  29.3 0.7 fusion.76
  30.0 0.6 fusion.77
  44.5 0.1 iota_compare_fusion.1
  44.7 6.4 %collective-permute-start.5 = (f32[2,48,1024]{2,1,0:T(8,128)S(1)}, f32[2,48,1024]{2,1,0:T(8,128)S(1)}, u32[]{:S(2)}, u32[]{:S(2)}) collective-permute-start(f32[2,48,1024]{2,1,0:T(8,128)S(1)} %copy-done.4), channel_id=1, source_target_pairs={{0,500},{4,504},{8,508},{12,0},{16,4},{20,8},{24,12},{28,16},{32,2... | collective-permute-start | bytes 1179656 | tf_op jit(solution)/shard_map/ppermute | solution.py:15
  51.0 1.0 constant_dynamic-update-slice_fusion.6
  52.1 7.3 %collective-permute-done.1 = f32[2,48,1024]{2,1,0:T(8,128)} collective-permute-done((f32[2,48,1024]{2,1,0:T(8,128)}, f32[2,48,1024]{2,1,0:T(8,128)}, u32[]{:S(2)}, u32[]{:S(2)}) %collective-permute-start.1) | collective-permute-done | bytes 393248 | tf_op jit(solution)/shard_map/ppermute | solution.py:15
  59.3 1.0 constant_dynamic-update-slice_fusion.5
  60.4 8.7 %collective-permute-done.2 = f32[2,48,1024]{2,1,0:T(8,128)} collective-permute-done((f32[2,48,1024]{2,1,0:T(8,128)}, f32[2,48,1024]{2,1,0:T(8,128)}, u32[]{:S(2)}, u32[]{:S(2)}) %collective-permute-start.2) | collective-permute-done | bytes 393248 | tf_op jit(solution)/shard_map/ppermute | solution.py:15
  69.1 1.0 constant_dynamic-update-slice_fusion.4
  70.1 1.0 constant_dynamic-update-slice_fusion.2
  71.4 0.3 fusion.34
  71.7 8.0 %collective-permute-start.6 = (f32[2,15,1024]{2,1,0:T(8,128)S(1)}, f32[2,15,1024]{2,1,0:T(8,128)S(1)}, u32[]{:S(2)}, u32[]{:S(2)}) collective-permute-start(f32[2,15,1024]{2,1,0:T(8,128)S(1)} %get-tuple-element.26), channel_id=1, source_target_pairs={{0,1},{1,2},{2,3},{4,5},{5,6},{6,7},{8,9},{9,10},{10,11},{12,13},{... | collective-permute-start | bytes 368648 | tf_op jit(solution)/shard_map/ppermute | solution.py:23
  79.7 2.1 collective-permute-start.7
  81.8 0.5 fusion.23
  82.4 3.5 %collective-permute-done.7 = f32[2,15,1024]{2,1,0:T(8,128)S(1)} collective-permute-done((f32[2,15,1024]{2,1,0:T(8,128)S(1)}, f32[2,15,1024]{2,1,0:T(8,128)S(1)}, u32[]{:S(2)}, u32[]{:S(2)}) %collective-permute-start.7) | collective-permute-done | bytes 122912 | tf_op jit(solution)/shard_map/ppermute | solution.py:26
  86.3 0.1 fusion.45
  86.4 0.1 fusion.44
  86.7 0.1 fusion.41
  86.9 24.3 %fusion.8 = f32[2,8,78,31,128]{4,2,1,0,3:T(8,128)} fusion(f32[158,128,31]{1,2,0:T(8,128)S(1)} %fusion.6, f32[2,8,78,158]{3,2,0,1:T(8,128)S(1)} %fusion.40), kind=kOutput, calls=%fused_computation.9 | convolution fusion | flops 9389113344 | bytes 23104768 | tf_op jit(solution)/shard_map/vnsw,wbc->vnsbc/dot_general | solution.py:98
  111.2 20.7 %convolution_bitcast_fusion = f32[2,8,31,48,128]{4,3,1,0,2:T(8,128)S(1)} fusion(f32[2,8,78,31,128]{4,2,1,0,3:T(8,128)} %fusion.8, f32[48,78,31]{1,2,0:T(8,128)S(1)} %fusion.23), kind=kOutput, calls=%fused_computation.6 | convolution fusion | flops 2852388864 | bytes 32462208 | tf_op jit(solution)/shard_map/bys,vnsbc->vnbyc/dot_general | solution.py:99
  131.9 41.4 %fusion.12 = f32[2,31,31]{1,2,0:T(8,128)S(1)} fusion(f32[2,8,31,48,128]{4,3,1,0,2:T(8,128)S(1)} %convolution_bitcast_fusion), kind=kOutput, calls=%fused_computation.14 | convolution fusion | flops 1133641728 | bytes 12197384 | tf_op jit(solution)/shard_map/vnbyc,vnjyc->vbj/dot_general | solution.py:101
  173.3 29.2 %fusion.2 = f32[2,1,31,1,1]{2,1,4,3,0:T(1,128)S(1)} fusion(f32[2,8,31,48,128]{4,3,1,0,2:T(8,128)S(1)} %convolution_bitcast_fusion, f32[2,48,8,128,1]{3,2,1,0,4:T(8,128)S(1)} %bitcast.167), kind=kOutput, calls=%fused_computation.2 | convolution fusion | flops 36569088 | bytes 12583160 | tf_op jit(solution)/shard_map/vnbyc,vync->vb/dot_general | solution.py:102
  202.5 10.5 %all-reduce.1 = (f32[2,31,31]{1,2,0:T(8,128)S(1)}, f32[2,31]{1,0:T(2,128)S(1)}) all-reduce(f32[2,31,31]{1,2,0:T(8,128)S(1)} %fusion.12, f32[2,31]{1,0:T(2,128)S(1)} %bitcast.170), channel_id=1, replica_groups=mesh['visit'=128,'quad'=4] {'quad'}, use_global_device_ids=true, to_apply=%region_0.1 | all-reduce | flops 1984 | bytes 15872 | tf_op jit(solution)/shard_map/psum | solution.py:103
  213.2 2.8 cholesky.44
  216.1 0.6 compare_reduce_fusion.1
  216.7 0.7 fusion.47
  217.4 2.4 custom-call.8
  219.8 0.2 convolution_bitcast_fusion.2
  219.9 0.1 fusion.55
  220.1 2.8 cholesky.55
  222.9 0.6 compare_reduce_fusion
  223.6 0.7 fusion.48
  224.2 2.4 custom-call.9
  226.6 0.2 convolution_bitcast_fusion.1
  226.8 0.1 fusion.51
  226.9 19.0 %fusion = f32[2,1,8,48,128]{4,1,3,2,0:T(1,128)S(1)} fusion(f32[2,31,1,1,1]{1,2,4,3,0:T(1,128)S(1)} %bitcast.171, f32[2,8,31,48,128]{4,3,1,0,2:T(8,128)} %copy-done.1), kind=kOutput, calls=%fused_computation | convolution fusion | flops 36569088 | bytes 12583160 | tf_op jit(solution)/shard_map/vb,vnbyc->vync/dot_general | solution.py:111
  246.0 0.1 copy.65
  246.3 1.3 dynamic_update_slice.6
  247.6 0.2 copy.22
  247.8 0.2 copy.23
  248.1 2.1 dynamic_update_slice.7
  250.2 0.2 copy.24
  250.4 0.1 stack.98
  250.6 2.3 fusion.15
  252.9 0.9 fusion.75
  253.8 1.9 collective-permute-start.10
  255.7 10.0 %collective-permute-start.11 = (f32[2,48,1024]{2,0,1:T(2,128)S(1)}, f32[2,48,1024]{2,0,1:T(2,128)S(1)}, u32[]{:S(2)}, u32[]{:S(2)}) collective-permute-start(f32[2,48,1024]{2,0,1:T(2,128)S(1)} %get-tuple-element.13), channel_id=1, source_target_pairs={{0,504},{4,508},{8,0},{12,4},{16,8},{20,12},{24,16},{28,20},{32,24... | collective-permute-start | bytes 1179656 | tf_op jit(solution)/shard_map/ppermute | solution.py:15
  265.7 1.9 collective-permute-start.12
  267.6 10.9 %collective-permute-start.13 = (f32[2,48,1024]{2,0,1:T(2,128)S(1)}, f32[2,48,1024]{2,0,1:T(2,128)S(1)}, u32[]{:S(2)}, u32[]{:S(2)}) collective-permute-start(f32[2,48,1024]{2,0,1:T(2,128)S(1)} %get-tuple-element.11), channel_id=1, source_target_pairs={{0,500},{4,504},{8,508},{12,0},{16,4},{20,8},{24,12},{28,16},{32,2... | collective-permute-start | bytes 1179656 | tf_op jit(solution)/shard_map/ppermute | solution.py:15
  278.5 1.9 collective-permute-start.8
  280.5 10.1 %collective-permute-start.9 = (f32[2,48,1024]{2,0,1:T(2,128)S(1)}, f32[2,48,1024]{2,0,1:T(2,128)S(1)}, u32[]{:S(2)}, u32[]{:S(2)}) collective-permute-start(f32[2,48,1024]{2,0,1:T(2,128)S(1)} %get-tuple-element.15), channel_id=1, source_target_pairs={{0,508},{4,0},{8,4},{12,8},{16,12},{20,16},{24,20},{28,24},{32,28}... | collective-permute-start | bytes 1179656 | tf_op jit(solution)/shard_map/ppermute | solution.py:15
  290.6 15.0 %collective-permute-done.12 = f32[2,48,1024]{2,0,1:T(2,128)S(1)} collective-permute-done((f32[2,48,1024]{2,0,1:T(2,128)S(1)}, f32[2,48,1024]{2,0,1:T(2,128)S(1)}, u32[]{:S(2)}, u32[]{:S(2)}) %collective-permute-start.12) | collective-permute-done | bytes 393248 | tf_op jit(solution)/shard_map/ppermute | solution.py:15
  305.5 2.1 collective-permute-done.13
  307.6 6.0 %collective-permute-done.8 = f32[2,48,1024]{2,0,1:T(2,128)S(1)} collective-permute-done((f32[2,48,1024]{2,0,1:T(2,128)S(1)}, f32[2,48,1024]{2,0,1:T(2,128)S(1)}, u32[]{:S(2)}, u32[]{:S(2)}) %collective-permute-start.8) | collective-permute-done | bytes 393248 | tf_op jit(solution)/shard_map/ppermute | solution.py:15
  313.7 2.4 collective-permute-done.9
  316.0 0.7 fusion.31
  316.7 0.9 copy.25
  (50 shorter events, 1.5 us)
Async XLA Ops:
  0.6 27.4 %copy-start = (f32[31,31]{1,0:T(8,128)S(1)}, f32[31,31]{1,0:T(8,128)}, u32[]{:S(2)}) copy-start(f32[31,31]{1,0:T(8,128)} %param.14) | copy-start | bytes 11536
  0.6 44.0 %copy-start.4 = (f32[2,48,1024]{2,1,0:T(8,128)S(1)}, f32[2,48,1024]{2,1,0:T(8,128)}, u32[]{:S(2)}) copy-start(f32[2,48,1024]{2,1,0:T(8,128)} %param.10) | copy-start | bytes 1179652
  0.7 28.7 %copy-start.6 = (s32[2,2]{1,0:T(2,128)S(1)}, s32[2,2]{1,0:T(2,128)}, u32[]{:S(2)}) copy-start(s32[2,2]{1,0:T(2,128)} %param.11) | copy-start | bytes 52
  0.7 29.3 %copy-start.7 = (s32[2]{0:T(128)S(1)}, s32[2]{0:T(128)}, u32[]{:S(2)}) copy-start(s32[2]{0:T(128)} %param.12) | copy-start | bytes 28
  0.7 44.0 %collective-permute-start = (f32[2,48,1024]{2,1,0:T(8,128)}, f32[2,48,1024]{2,1,0:T(8,128)}, u32[]{:S(2)}, u32[]{:S(2)}) collective-permute-start(f32[2,48,1024]{2,1,0:T(8,128)} %param.10), channel_id=1, source_target_pairs={{0,12},{4,16},{8,20},{12,24},{16,28},{20,32},{24,36},{28,40},{32,4... | collective-permute-start | bytes 1179656 | tf_op jit(solution)/shard_map/ppermute | solution.py:15
  6.9 52.5 %collective-permute-start.1 = (f32[2,48,1024]{2,1,0:T(8,128)}, f32[2,48,1024]{2,1,0:T(8,128)}, u32[]{:S(2)}, u32[]{:S(2)}) collective-permute-start(f32[2,48,1024]{2,1,0:T(8,128)} %param.10), channel_id=1, source_target_pairs={{0,8},{4,12},{8,16},{12,20},{16,24},{20,28},{24,32},{28,36},{32,40... | collective-permute-start | bytes 1179656 | tf_op jit(solution)/shard_map/ppermute | solution.py:15
  11.4 57.6 %collective-permute-start.2 = (f32[2,48,1024]{2,1,0:T(8,128)}, f32[2,48,1024]{2,1,0:T(8,128)}, u32[]{:S(2)}, u32[]{:S(2)}) collective-permute-start(f32[2,48,1024]{2,1,0:T(8,128)} %param.10), channel_id=1, source_target_pairs={{0,4},{4,8},{8,12},{12,16},{16,20},{20,24},{24,28},{28,32},{32,36}... | collective-permute-start | bytes 1179656 | tf_op jit(solution)/shard_map/ppermute | solution.py:15
  13.7 56.4 %collective-permute-start.3 = (f32[2,48,1024]{2,1,0:T(8,128)}, f32[2,48,1024]{2,1,0:T(8,128)}, u32[]{:S(2)}, u32[]{:S(2)}) collective-permute-start(f32[2,48,1024]{2,1,0:T(8,128)} %param.10), channel_id=1, source_target_pairs={{0,508},{4,0},{8,4},{12,8},{16,12},{20,16},{24,20},{28,24},{32,28}... | collective-permute-start | bytes 1179656 | tf_op jit(solution)/shard_map/ppermute | solution.py:15
  23.5 47.7 %collective-permute-start.4 = (f32[2,48,1024]{2,1,0:T(8,128)}, f32[2,48,1024]{2,1,0:T(8,128)S(1)}, u32[]{:S(2)}, u32[]{:S(2)}) collective-permute-start(f32[2,48,1024]{2,1,0:T(8,128)} %param.10), channel_id=1, source_target_pairs={{0,504},{4,508},{8,0},{12,4},{16,8},{20,12},{24,16},{28,20},{32,24... | collective-permute-start | bytes 1179656 | tf_op jit(solution)/shard_map/ppermute | solution.py:15
  44.7 26.6 %collective-permute-start.5 = (f32[2,48,1024]{2,1,0:T(8,128)S(1)}, f32[2,48,1024]{2,1,0:T(8,128)S(1)}, u32[]{:S(2)}, u32[]{:S(2)}) collective-permute-start(f32[2,48,1024]{2,1,0:T(8,128)S(1)} %copy-done.4), channel_id=1, source_target_pairs={{0,500},{4,504},{8,508},{12,0},{16,4},{20,8},{24,12},{28,16},{32,2... | collective-permute-start | bytes 1179656 | tf_op jit(solution)/shard_map/ppermute | solution.py:15
  70.1 11.7 %copy-start.5 = (f32[31,31]{1,0:T(8,128)S(1)}, f32[31,31]{1,0:T(8,128)}, u32[]{:S(2)}) copy-start(f32[31,31]{1,0:T(8,128)} %param.13) | copy-start | bytes 11536
  71.2 11.1 %copy-start.2 = (f32[2,48,1024]{2,1,0:T(8,128)S(1)}, f32[2,48,1024]{2,1,0:T(8,128)}, u32[]{:S(2)}) copy-start(f32[2,48,1024]{2,1,0:T(8,128)} %param.9) | copy-start | bytes 1179652
  71.7 10.8 %collective-permute-start.6 = (f32[2,15,1024]{2,1,0:T(8,128)S(1)}, f32[2,15,1024]{2,1,0:T(8,128)S(1)}, u32[]{:S(2)}, u32[]{:S(2)}) collective-permute-start(f32[2,15,1024]{2,1,0:T(8,128)S(1)} %get-tuple-element.26), channel_id=1, source_target_pairs={{0,1},{1,2},{2,3},{4,5},{5,6},{6,7},{8,9},{9,10},{10,11},{12,13},{... | collective-permute-start | bytes 368648 | tf_op jit(solution)/shard_map/ppermute | solution.py:23
  79.7 6.3 %collective-permute-start.7 = (f32[2,15,1024]{2,1,0:T(8,128)S(1)}, f32[2,15,1024]{2,1,0:T(8,128)S(1)}, u32[]{:S(2)}, u32[]{:S(2)}) collective-permute-start(f32[2,15,1024]{2,1,0:T(8,128)S(1)} %get-tuple-element.27), channel_id=1, source_target_pairs={{1,0},{2,1},{3,2},{5,4},{6,5},{7,6},{9,8},{10,9},{11,10},{13,12},{... | collective-permute-start | bytes 368648 | tf_op jit(solution)/shard_map/ppermute | solution.py:26
  131.9 41.4 %copy-start.1 = (f32[2,8,31,48,128]{4,3,1,0,2:T(8,128)}, f32[2,8,31,48,128]{4,3,1,0,2:T(8,128)S(1)}, u32[]{:S(2)}) copy-start(f32[2,8,31,48,128]{4,3,1,0,2:T(8,128)S(1)} %convolution_bitcast_fusion) | copy-start | bytes 36569092
  246.2 4.3 %copy-start.3 = (f32[2,48,1024]{2,1,0:T(8,128)}, f32[2,48,1024]{2,1,0:T(8,128)S(1)}, u32[]{:S(2)}) copy-start(f32[2,48,1024]{2,1,0:T(8,128)S(1)} %sub.60) | copy-start | bytes 1179652
  253.8 26.7 %collective-permute-start.10 = (f32[2,48,1024]{2,0,1:T(2,128)S(1)}, f32[2,48,1024]{2,0,1:T(2,128)S(1)}, u32[]{:S(2)}, u32[]{:S(2)}) collective-permute-start(f32[2,48,1024]{2,0,1:T(2,128)S(1)} %get-tuple-element.14), channel_id=1, source_target_pairs={{0,8},{4,12},{8,16},{12,20},{16,24},{20,28},{24,32},{28,36},{32,40... | collective-permute-start | bytes 1179656 | tf_op jit(solution)/shard_map/ppermute | solution.py:15
  255.7 34.8 %collective-permute-start.11 = (f32[2,48,1024]{2,0,1:T(2,128)S(1)}, f32[2,48,1024]{2,0,1:T(2,128)S(1)}, u32[]{:S(2)}, u32[]{:S(2)}) collective-permute-start(f32[2,48,1024]{2,0,1:T(2,128)S(1)} %get-tuple-element.13), channel_id=1, source_target_pairs={{0,504},{4,508},{8,0},{12,4},{16,8},{20,12},{24,16},{28,20},{32,24... | collective-permute-start | bytes 1179656 | tf_op jit(solution)/shard_map/ppermute | solution.py:15
  265.7 39.8 %collective-permute-start.12 = (f32[2,48,1024]{2,0,1:T(2,128)S(1)}, f32[2,48,1024]{2,0,1:T(2,128)S(1)}, u32[]{:S(2)}, u32[]{:S(2)}) collective-permute-start(f32[2,48,1024]{2,0,1:T(2,128)S(1)} %get-tuple-element.12), channel_id=1, source_target_pairs={{0,12},{4,16},{8,20},{12,24},{16,28},{20,32},{24,36},{28,40},{32,4... | collective-permute-start | bytes 1179656 | tf_op jit(solution)/shard_map/ppermute | solution.py:15
  267.6 40.0 %collective-permute-start.13 = (f32[2,48,1024]{2,0,1:T(2,128)S(1)}, f32[2,48,1024]{2,0,1:T(2,128)S(1)}, u32[]{:S(2)}, u32[]{:S(2)}) collective-permute-start(f32[2,48,1024]{2,0,1:T(2,128)S(1)} %get-tuple-element.11), channel_id=1, source_target_pairs={{0,500},{4,504},{8,508},{12,0},{16,4},{20,8},{24,12},{28,16},{32,2... | collective-permute-start | bytes 1179656 | tf_op jit(solution)/shard_map/ppermute | solution.py:15
  278.5 35.1 %collective-permute-start.8 = (f32[2,48,1024]{2,0,1:T(2,128)S(1)}, f32[2,48,1024]{2,0,1:T(2,128)S(1)}, u32[]{:S(2)}, u32[]{:S(2)}) collective-permute-start(f32[2,48,1024]{2,0,1:T(2,128)S(1)} %get-tuple-element.10), channel_id=1, source_target_pairs={{0,4},{4,8},{8,12},{12,16},{16,20},{20,24},{24,28},{28,32},{32,36}... | collective-permute-start | bytes 1179656 | tf_op jit(solution)/shard_map/ppermute | solution.py:15
  280.5 35.6 %collective-permute-start.9 = (f32[2,48,1024]{2,0,1:T(2,128)S(1)}, f32[2,48,1024]{2,0,1:T(2,128)S(1)}, u32[]{:S(2)}, u32[]{:S(2)}) collective-permute-start(f32[2,48,1024]{2,0,1:T(2,128)S(1)} %get-tuple-element.15), channel_id=1, source_target_pairs={{0,508},{4,0},{8,4},{12,8},{16,12},{20,16},{24,20},{28,24},{32,28}... | collective-permute-start | bytes 1179656 | tf_op jit(solution)/shard_map/ppermute | solution.py:15
where the time goes:
time: 319 us; the launch traced here: 318 us
  matrix products  139 us (44%)
  starting transfers between devices  80.2 us (25%)
  waiting for transfers between devices  45 us (14%)
  between operations  15.2 us (5%)
  other arithmetic  14.7 us (5%)
  local copies, waits for them, and re-layouts  12.8 us (4%)
  blocking collectives  10.5 us (3%)
    ppermute x12, starting transfers between devices, passed_along(): return lax.ppermute(x, axis, [(i, (i + by) % count) for i in range(count)])  70.1 us
    ppermute x12, waiting for transfers between devices, passed_along(): return lax.ppermute(x, axis, [(i, (i + by) % count) for i in range(count)])  41.5 us
    dot_general x1, matrix products, on_device(): normals = jnp.einsum('vnbyc,vnjyc->vbj', images, images, precision=HIGHEST)  41.4 us
    dot_general x1, matrix products, on_device(): moments = jnp.einsum('vnbyc,vync->vb', images, target, precision=HIGHEST)  29.2 us
    dot_general x1, matrix products, on_device(): jnp.einsum('vnsw,wbc->vnsbc', segments, band, precision=HIGHEST)  24.3 us
    dot_general x1, matrix products, on_device(): jnp.einsum('bys,vnsbc->vnbyc', weights, along_cols, precision=HIGHEST)  20.7 us
    dot_general x1, matrix products, on_device(): jnp.einsum('vb,vnbyc->vync', coefficients, images, precision=HIGHEST)  19 us
    psum x1, blocking collectives, on_device(): normal_sum, moment_sum = lax.psum((normals, moments), 'quad')  10.5 us
  transfers between devices with their start and end apart: 14, of which 7 were waited for; matrix products, arithmetic and copies ran while one was open for 2% of the time, Pallas kernels for 0%

commit v1 on v0

v1 whole, which is shorter than its diff:
```python
import functools

import jax
import jax.numpy as jnp
from jax import lax
from jax.experimental import pallas as pl
from jax.experimental.pallas import tpu as pltpu
from jax.sharding import PartitionSpec as P

MESH = pl.DeviceIdType.MESH
REACH = 3
LANES = 128
HALO = 16
EXT = 80
HIGHEST = lax.Precision.HIGHEST
F32 = jnp.float32
BF16 = jnp.bfloat16
SIGN = (1, -1)


def split(x):
    high = x.astype(BF16)
    return high, (x - high.astype(F32)).astype(BF16)


def kernel(
    pixels,
    sci, tiles, pairs, offs, brow, bcol,
    diff, coadd,
    metas, t1, snd2, r2, r3, pre, halo, tst, rmat, base, bmat, yhi, ylo, img,
    gacc, gbuf, cs, dt, dbank,
    ms, mr, s1, v1, s2, v2, s3, v3, hs, hr, gs, gr, ds_, dr,
):
    slots, rows, cols = sci.shape
    taps = 31
    count = 31
    half = rows // 2
    nv, nq = lax.axis_size("visit"), lax.axis_size("quad")
    me, q = lax.axis_index("visit"), lax.axis_index("quad")
    blocks = cols // LANES
    groups = half // 8

    def at_visit(step):
        return lax.rem(me + step + nv, nv)

    def at_quad(step):
        return lax.rem(q + step, nq)

    def remote(src, dst, send, recv, device):
        return pltpu.make_async_remote_copy(
            src_ref=src, dst_ref=dst, send_sem=send, recv_sem=recv,
            device_id=device, device_id_type=MESH,
        )

    steps = [step * sign for step in range(1, REACH + 1) for sign in SIGN]
    barrier = pltpu.get_barrier_semaphore()
    for step in steps:
        pl.semaphore_signal(barrier, inc=1, device_id={"visit": at_visit(step)}, device_id_type=MESH)
    for step in range(1, nq):
        pl.semaphore_signal(barrier, inc=1, device_id={"quad": at_quad(step)}, device_id_type=MESH)

    line = lax.broadcasted_iota(jnp.int32, (8, LANES), 0)
    own = jnp.zeros((8, LANES), jnp.int32)
    for slot in range(slots):
        for place, value in enumerate((pairs[slot, 0], pairs[slot, 1], offs[slot])):
            own = jnp.where(line == 3 * slot + place, value, own)
    metas[REACH] = own
    pl.semaphore_wait(barrier, len(steps) + nq - 1)

    meta_copies = [
        remote(metas.at[REACH], metas.at[REACH - step], ms.at[REACH - step], mr.at[REACH - step],
               {"visit": at_visit(step)})
        for step in steps
    ]
    for copy in meta_copies:
        copy.start()
    ahead = [{"visit": at_visit(sign)} for sign in SIGN]
    hop1 = [
        remote(tiles.at[t], t1.at[d, t], s1.at[d, t], v1.at[d, t], ahead[d])
        for t in range(slots) for d in range(2)
    ]
    for copy in hop1:
        copy.start()

    tst[...] = jnp.zeros_like(tst)
    bmat[...] = jnp.zeros_like(bmat)
    blank = jnp.zeros((32, LANES), F32)
    row_high = brow[...].astype(BF16).astype(F32)
    row_low = brow[...] - row_high
    wide_high = jnp.concatenate([row_high, blank], axis=1)
    wide_low = jnp.concatenate([row_low, blank], axis=1)
    base[0] = (
        pltpu.roll(wide_high, 1, 1) + pltpu.roll(wide_low, EXT + 1, 1) + pltpu.roll(wide_high, 2 * EXT + 1, 1)
    )
    col_high = bcol[...].astype(BF16).astype(F32)
    back = 2 * LANES - (taps - 1)
    base[1] = pltpu.roll(jnp.concatenate([col_high, blank], axis=1), back, 1)
    base[2] = pltpu.roll(jnp.concatenate([bcol[...] - col_high, blank], axis=1), back, 1)

    @pl.loop(0, count)
    def _(k):
        first = pl.multiple_of(k * rows, 16)
        line_k = jnp.broadcast_to(base[0, pl.ds(k, 1), :], (rows, 2 * LANES))
        rmat[pl.ds(first, rows), :] = pltpu.roll(line_k, 0, 1, stride=1, stride_axis=0).astype(BF16)
        for part in range(2):
            line_k = jnp.broadcast_to(base[1 + part, pl.ds(k, 1), :], (EXT, 2 * LANES))
            band = pltpu.roll(line_k, 0, 1, stride=1, stride_axis=0)
            for piece in range(2):
                if piece:
                    band = pltpu.roll(band, EXT, 1)
                bmat[k, piece * EXT:(piece + 1) * EXT, part * LANES:(part + 1) * LANES] = (
                    band[:, :LANES].astype(BF16)
                )

    @pl.when(q == 0)
    def _():
        for slot in range(slots):
            halo[slot, 0] = jnp.zeros((HALO, cols), F32)

    @pl.when(q == nq - 1)
    def _():
        for slot in range(slots):
            halo[slot, 1] = jnp.zeros((HALO, cols), F32)

    for copy in meta_copies:
        copy.wait()

    column = lax.broadcasted_iota(jnp.int32, (8, cols), 1)

    def owner(step, slot):
        def wide(place):
            value = metas[REACH + step, 3 * slot + place:3 * slot + place + 1, :]
            return jnp.concatenate([jnp.broadcast_to(value, (8, LANES))] * blocks, axis=1)
        return jnp.where(column >= wide(2), wide(0), wide(1))

    def group(part, g):
        return pl.ds(part * half + g * 8, 8)

    def part_rows(part):
        return pl.ds(part * half, half)

    for copy in hop1:
        copy.wait_recv()

    def second(d, slot, part):
        return remote(snd2.at[d, slot, part_rows(part)], r2.at[d, slot, part_rows(part)],
                      s2.at[d, slot, part], v2.at[d, slot, part], ahead[d])

    def third(d, slot, part):
        return remote(r2.at[d, slot, part_rows(part)], r3.at[d, slot, part_rows(part)],
                      s3.at[d, slot, part], v3.at[d, slot, part], ahead[d])

    def build(slot, part):
        for d, sign in enumerate(SIGN):
            wanted = owner(2 * sign, slot)
            source = at_visit(-sign)
            for g in range(groups):
                total = jnp.zeros((8, cols), F32)
                for t in range(slots):
                    total = jnp.where(wanted == slots * me + t, tiles[t, group(part, g), :], total)
                    total = jnp.where(wanted == slots * source + t, t1[d, t, group(part, g), :], total)
                snd2[d, slot, group(part, g), :] = total

    def start_second(slot, part):
        for d in range(2):
            second(d, slot, part).start()

    def relay(slot, part):
        for d, sign in enumerate(SIGN):
            wanted = owner(sign, slot)
            second(d, slot, part).wait_recv()
            for g in range(groups):
                total = r2[d, slot, group(part, g), :]
                for t in range(slots):
                    total = jnp.where(wanted == slots * me + t, tiles[t, group(part, g), :], total)
                r2[d, slot, group(part, g), :] = total
            third(d, slot, part).start()

    for part in range(2):
        build(0, part)
        start_second(0, part)
    for part in range(2):
        build(1, part)
    for part in range(2):
        relay(0, part)
    for part in range(2):
        start_second(1, part)

    def halo_copies(slot):
        down = remote(pre.at[slot, pl.ds(rows - HALO, HALO)], halo.at[slot, 0],
                      hs.at[slot, 0], hr.at[slot, 0], {"quad": at_quad(1)})
        up = remote(pre.at[slot, pl.ds(0, HALO)], halo.at[slot, 1],
                    hs.at[slot, 1], hr.at[slot, 1], {"quad": at_quad(nq - 1)})
        return down, up

    lane = lax.broadcasted_iota(jnp.int32, (HALO, LANES), 1)

    def spread(x, slot, first):
        shift = lax.rem(cols + taps // 2 - offs[slot], cols)
        x = pltpu.roll(x, shift, 1)
        head = x[:, :LANES]
        ext = jnp.concatenate(
            [jnp.where(lane >= taps // 2, head, 0.0), x[:, LANES:], jnp.where(lane < taps // 2, head, 0.0)],
            axis=1,
        )
        high, low = split(ext)
        width = cols + LANES
        tst[first:first + HALO, :width] = high
        tst[EXT + first:EXT + first + HALO, :width] = high
        tst[2 * EXT + first:2 * EXT + first + HALO, :width] = low

    own_row = lax.broadcasted_iota(jnp.int32, (32, LANES), 0)
    own_col = lax.broadcasted_iota(jnp.int32, (32, LANES), 1)

    def convolve(slot, events):
        for part in range(2):
            for d in range(2):
                third(d, slot, part).wait_recv()
        wanted = owner(0, slot)
        for g in range(rows // 8):
            sl = pl.ds(g * 8, 8)
            total = r3[0, slot, sl, :] + r3[1, slot, sl, :]
            for t in range(slots):
                total = jnp.where(wanted == slots * me + t, tiles[t, sl, :], total)
            pre[slot, sl, :] = total
        down, up = halo_copies(slot)

        @pl.when(q < nq - 1)
        def _():
            down.start()

        @pl.when(q > 0)
        def _():
            up.start()

        for g in range(rows // HALO):
            spread(pre[slot, g * HALO:(g + 1) * HALO, :], slot, HALO + g * HALO)

        @pl.when(q > 0)
        def _():
            down.wait_recv()

        @pl.when(q < nq - 1)
        def _():
            up.wait_recv()

        spread(halo[slot, 0], slot, 0)
        spread(halo[slot, 1], slot, HALO + rows)
        events[0]()

        chunk = count * HALO

        @pl.loop(0, (cols + 2 * LANES) // (2 * LANES))
        def _(n):
            sl = pl.ds(pl.multiple_of(n * 2 * LANES, 2 * LANES), 2 * LANES)
            weight = tst[:, sl]
            for piece in range(count * rows // chunk):
                rsl = pl.ds(piece * chunk, chunk)
                high, low = split(jnp.dot(rmat[rsl, :], weight, preferred_element_type=F32))
                yhi[rsl, sl] = high
                ylo[rsl, sl] = low

        events[1]()
        bounds = (0, 8, 16, 24, count)
        for segment in range(4):
            @pl.loop(bounds[segment], bounds[segment + 1])
            def _(k):
                rsl = pl.ds(pl.multiple_of(k * rows, 16), rows)
                left = jnp.concatenate(
                    [y[rsl, n * LANES:(n + 2) * LANES] for y in (yhi, ylo) for n in range(blocks)], axis=0
                )
                out = jnp.dot(left, bmat[k], preferred_element_type=F32)
                out = out[:, :LANES] + out[:, LANES:]
                out = out[:rows * blocks] + out[rows * blocks:]
                for n in range(blocks):
                    img[k, :, n * LANES:(n + 1) * LANES] = out[n * rows:(n + 1) * rows]
            events[2 + segment]()

        img[count] = sci[slot]
        gacc[...] = jnp.zeros_like(gacc)

        @pl.loop(0, rows // 8)
        def _(g):
            x = img[:, pl.ds(pl.multiple_of(g * 8, 8), 8), :].reshape(256, cols)
            high, low = split(x)
            both = jnp.concatenate([high, low], axis=0)
            gacc[...] += lax.dot_general(high, both, (((1,), (1,)), ((), ())), preferred_element_type=F32)

        srow = lax.broadcasted_iota(jnp.int32, (256, 256), 0)
        scol = lax.broadcasted_iota(jnp.int32, (256, 256), 1)
        same = lax.rem(srow, 8) == lax.rem(scol, 8)
        prow = lax.broadcasted_iota(jnp.int32, (256, LANES), 0)
        pcol = lax.broadcasted_iota(jnp.int32, (256, LANES), 1)
        gather = (lax.div(prow, 8) == pcol).astype(F32)

        def reduced(x):
            x = jnp.where(same, x, 0.0).reshape(32, 8, 256).sum(axis=1)
            return jnp.dot(x, gather, precision=HIGHEST, preferred_element_type=F32)

        main = reduced(gacc[:, :256])
        cross = reduced(gacc[:, 256:])
        square = jnp.concatenate([cross, jnp.zeros((96, LANES), F32)], axis=0)
        gbuf[slot, 0] = main + cross + square.T[:32]
        copies = [
            remote(gbuf.at[slot, 0], gbuf.at[slot, step], gs.at[slot, step - 1], gr.at[slot, step - 1],
                   {"quad": at_quad(step)})
            for step in range(1, nq)
        ]
        for copy in copies:
            copy.start()
        events[6]()
        for copy in copies:
            copy.wait_recv()
        total = gbuf[slot, lax.rem(q + nq, nq)]
        for source in range(1, nq):
            total = total + gbuf[slot, lax.rem(q + nq - source, nq)]
        system = total / pixels + jnp.where((own_row == own_col) & (own_col < count), 0.01, 0.0)
        for j in range(count):
            pivot_row = system[j:j + 1, :]
            pivot_col = jnp.broadcast_to(system[:, j:j + 1], (32, LANES))
            pivot = jnp.broadcast_to(system[j:j + 1, j:j + 1], (1, LANES))
            scaled = pivot_row * (1.0 / pivot)
            system = jnp.where(own_row == j, scaled, system - pivot_col * scaled)
        cs[...] = jnp.broadcast_to(system[:, count:count + 1], (32, LANES))

        @pl.loop(0, rows // 8)
        def _(g):
            sl = pl.ds(pl.multiple_of(g * 8, 8), 8)
            total = sci[slot, sl, :]
            for k in range(count):
                weight = jnp.broadcast_to(cs[k:k + 1, :], (8, LANES))
                total = total - jnp.concatenate([weight] * blocks, axis=1) * img[k, sl, :]
            diff[slot, sl, :] = total
            dt[slot, sl, :] = pltpu.roll(total, offs[slot], 1)

    def spread_copy(d, hop, slot, part):
        source = dt.at[slot, part_rows(part)] if hop == 0 else dbank.at[d, hop - 1, slot, part_rows(part)]
        return remote(source, dbank.at[d, hop, slot, part_rows(part)],
                      ds_.at[d, hop, slot, part], dr.at[d, hop, slot, part], ahead[d])

    def start_spread(slot):
        for part in range(2):
            for d in range(2):
                spread_copy(d, 0, slot, part).start()

    def forward(hop, slot, part):
        for d in range(2):
            spread_copy(d, hop, slot, part).wait_recv()
            if hop + 1 < REACH:
                spread_copy(d, hop + 1, slot, part).start()

    def add(step, slot, data, parts=(0, 1)):
        wanted = owner(step, slot)
        for part in parts:
            for g in range(groups):
                value = data[group(part, g), :]
                for t in range(slots):
                    coadd[t, group(part, g), :] += jnp.where(wanted == slots * me + t, value, 0.0)

    def nothing():
        pass

    relay_events = [nothing] * 7
    relay_events[1] = functools.partial(relay, 1, 0)
    relay_events[2] = functools.partial(relay, 1, 1)
    convolve(0, relay_events)
    start_spread(0)
    for t in range(slots):
        coadd[t] = jnp.zeros((rows, cols), F32)
    add(0, 0, dt.at[0])

    spread_events = [nothing] * 7
    spread_events[1] = functools.partial(forward, 0, 0, 0)
    spread_events[2] = functools.partial(forward, 0, 0, 1)
    spread_events[3] = functools.partial(forward, 1, 0, 0)
    spread_events[4] = functools.partial(forward, 1, 0, 1)
    convolve(1, spread_events)
    start_spread(1)
    add(0, 1, dt.at[1])
    for d, sign in enumerate(SIGN):
        add(-sign, 0, dbank.at[d, 0, 0])
    forward(0, 1, 0)
    forward(0, 1, 1)
    for d, sign in enumerate(SIGN):
        add(-2 * sign, 0, dbank.at[d, 1, 0])
    forward(1, 1, 0)
    forward(1, 1, 1)
    forward(2, 0, 0)
    forward(2, 0, 1)
    for d, sign in enumerate(SIGN):
        add(-3 * sign, 0, dbank.at[d, 2, 0])
        add(-sign, 1, dbank.at[d, 0, 1])
        add(-2 * sign, 1, dbank.at[d, 1, 1])
    for part in range(2):
        forward(2, 1, part)
        for d, sign in enumerate(SIGN):
            add(-3 * sign, 1, dbank.at[d, 2, 1], (part,))

    for copy in hop1:
        copy.wait_send()
    for slot in range(slots):
        down, up = halo_copies(slot)

        @pl.when(q < nq - 1)
        def _():
            down.wait_send()

        @pl.when(q > 0)
        def _():
            up.wait_send()

        for step in range(1, nq):
            remote(gbuf.at[slot, 0], gbuf.at[slot, step], gs.at[slot, step - 1], gr.at[slot, step - 1],
                   {"quad": at_quad(step)}).wait_send()
        for part in range(2):
            for d in range(2):
                second(d, slot, part).wait_send()
                third(d, slot, part).wait_send()
                for hop in range(REACH):
                    spread_copy(d, hop, slot, part).wait_send()


def on_device(science, reference_tiles, visit_tiles, offsets, basis_rows, basis_cols):
    slots, rows, cols = science.shape
    count = basis_rows.shape[0]
    nq = lax.axis_size("quad")
    pixels = nq * rows * cols
    pad = ((0, 32 - count), (0, LANES - basis_rows.shape[1]))
    brow = jnp.pad(basis_rows, pad)
    bcol = jnp.pad(basis_cols[:, ::-1], pad)
    vmem = pl.BlockSpec(memory_space=pltpu.VMEM)
    smem = pl.BlockSpec(memory_space=pltpu.SMEM)
    dma = pltpu.SemaphoreType.DMA
    ext_cols = cols + 2 * LANES
    return pl.pallas_call(
        functools.partial(kernel, float(pixels)),
        out_shape=[jax.ShapeDtypeStruct((slots, rows, cols), F32)] * 2,
        in_specs=[vmem, vmem, smem, smem, vmem, vmem],
        out_specs=[vmem, vmem],
        scratch_shapes=[
            pltpu.VMEM((2 * REACH + 1, 8, LANES), jnp.int32),
            pltpu.VMEM((2, slots, rows, cols), F32),
            pltpu.VMEM((2, slots, rows, cols), F32),
            pltpu.VMEM((2, slots, rows, cols), F32),
            pltpu.VMEM((2, slots, rows, cols), F32),
            pltpu.VMEM((slots, rows, cols), F32),
            pltpu.VMEM((slots, 2, HALO, cols), F32),
            pltpu.VMEM((256, ext_cols), BF16),
            pltpu.VMEM((count * rows, 256), BF16),
            pltpu.VMEM((3, 32, 256), F32),
            pltpu.VMEM((count, 256, 256), BF16),
            pltpu.VMEM((count * rows, ext_cols), BF16),
            pltpu.VMEM((count * rows, ext_cols), BF16),
            pltpu.VMEM((count + 1, rows, cols), F32),
            pltpu.VMEM((256, 512), F32),
            pltpu.VMEM((slots, nq, 32, LANES), F32),
            pltpu.VMEM((32, LANES), F32),
            pltpu.VMEM((slots, rows, cols), F32),
            pltpu.VMEM((2, REACH, slots, rows, cols), F32),
            dma((2 * REACH + 1,)), dma((2 * REACH + 1,)),
            dma((2, slots)), dma((2, slots)),
            dma((2, slots, 2)), dma((2, slots, 2)),
            dma((2, slots, 2)), dma((2, slots, 2)),
            dma((slots, 2)), dma((slots, 2)),
            dma((slots, nq - 1)), dma((slots, nq - 1)),
            dma((2, REACH, slots, 2)), dma((2, REACH, slots, 2)),
        ],
        compiler_params=pltpu.CompilerParams(
            collective_id=0, has_side_effects=True, vmem_limit_bytes=56 * 1024 * 1024
        ),
        cost_estimate=pl.CostEstimate(flops=8_000_000_000, bytes_accessed=2_000_000, transcendentals=0),
    )(science, reference_tiles, visit_tiles, offsets, brow, bcol)


def solution(mesh):
    tiles = P("visit", "quad", None)
    return jax.shard_map(
        on_device,
        mesh=mesh,
        in_specs=(tiles, tiles, P("visit", None), P("visit"), P(), P()),
        out_specs=(tiles, tiles),
        check_vma=False,
    )
```

time: 319 us -> 136 us (0.43)
  matrix products: 139 us -> 0 us
  Pallas kernels: 0 us -> 130 us
  starting transfers between devices: 80.2 us -> 0 us
  waiting for transfers between devices: 45 us -> 0 us
  other arithmetic: 14.7 us -> 0 us
  between operations: 15.2 us -> 0.66 us
  blocking collectives: 10.5 us -> 0 us
  local copies, waits for them, and re-layouts: 12.8 us -> 4.59 us
    dot_general x8 -> x0, matrix products: 139 us -> none  [the longest x1 41.4 us: on_device(): normals = jnp.einsum('vnbyc,vnjyc->vbj', images, images, precision=HIGHEST)]
    pallas_call x0 -> x1, Pallas kernels: none -> 130 us  [on_device(): pl.pallas_call(functools.partial(kernel, float(pixels)), out_shape=[jax.S...]
    ppermute x14 -> x0, starting transfers between devices: 80.2 us -> none  [the longest x12 70.1 us: passed_along(): return lax.ppermute(x, axis, [(i, (i + by) % count) for i in range(count)])]
    ppermute x14 -> x0, waiting for transfers between devices: 45 us -> none  [the longest x12 41.5 us: passed_along(): return lax.ppermute(x, axis, [(i, (i + by) % count) for i in range(count)])]
    another operation x13 -> x0, other arithmetic: 13.4 us -> none  [the longest x6 7.01 us: on_device(): factor = jnp.linalg.cholesky(system)]
    psum x1 -> x0, blocking collectives: 10.5 us -> none  [on_device(): normal_sum, moment_sum = lax.psum((normals, moments), 'quad')]
    dynamic_update_slice x2 -> x0, local copies, waits for them, and re-layouts: 3.35 us -> none  [on_device(): lax.dynamic_update_slice(jnp.zeros((local_rows, 2 * col_count), jnp.float...]
    unnamed x31 -> x6, local copies, waits for them, and re-layouts: 5.86 us -> 2.57 us
  transfers between devices with their start and end apart: 14 -> 0, of which waited for: 7 -> 0; matrix products, arithmetic and copies ran while one was open for 2% -> 0% of each run, Pallas kernels for 0% -> 0%
where the time goes in v1:
time: 136 us
  Pallas kernels  130 us (96%)
  local copies, waits for them, and re-layouts  4.59 us (3%)
    pallas_call x1, Pallas kernels, on_device(): pl.pallas_call(functools.partial(kernel, float(pixels)), out_shape=[jax.S...  130 us

profile of v1, /device:TPU:1, one launch (start us, length us, event | category | flops | bytes accessed | tf_op | source)
XLA Modules:
  0.0 135.5 jit_solution(1271678499193519847)
XLA Ops:
  0.6 0.0 copy-start.1
  0.6 1.3 pad.7.brow
  2.0 0.0 copy-done.1
  2.0 0.1 rev.3
  2.0 0.6 pad.8.bcol
  2.7 130.3 %shard_map.77 = (f32[2,48,1024]{2,1,0:T(8,128)}, f32[2,48,1024]{2,1,0:T(8,128)}) custom-call(f32[2,48,1024]{2,1,0:T(8,128)} %sci.1, f32[2,48,1024]{2,1,0:T(8,128)} %tiles.1, s32[2,2]{1,0:T(2,128)} %pairs.1, s32[2]{0:T(128)} %offs.1, f32[32,128]{1,0:T(8,128)} %pad.7.brow, f32[32,128]{1,0:T(8,128)} %pad.8.bcol), custom_call_target="tpu_custom_call" | custom-call | flops 8000000000 | bytes 2000000 | tf_op jit(solution)/shard_map/pallas_call | solution.py:435
  132.9 0.0 copy-start
  132.9 1.8 %copy.10 = f32[2,48,1024]{2,1,0:T(8,128)} copy(f32[2,48,1024]{2,1,0:T(8,128)} %get-tuple-element.4) | data formatting | bytes 786432
  134.8 0.0 copy-done
  134.8 0.7 copy.11
Async XLA Ops:
  0.6 1.3 copy-start.1
  132.9 1.8 %copy-start = (f32[2,48,1024]{2,1,0:T(8,128)S(1)}, f32[2,48,1024]{2,1,0:T(8,128)}, u32[]{:S(2)}) copy-start(f32[2,48,1024]{2,1,0:T(8,128)} %get-tuple-element.5) | copy-start | bytes 1179652

commit v2 on v1

--- a/solution.py
+++ b/solution.py
@@ -11,6 +11,7 @@
 REACH = 3
 LANES = 128
 HALO = 16
+CHUNKS = 3
 EXT = 80
 HIGHEST = lax.Precision.HIGHEST
 F32 = jnp.float32
@@ -27,18 +28,18 @@
     pixels,
     sci, tiles, pairs, offs, brow, bcol,
     diff, coadd,
-    metas, t1, snd2, r2, r3, pre, halo, tst, rmat, base, bmat, yhi, ylo, img,
+    metas, bank, pre, halo, tst, rmat, base, bmat, yhi, ylo, img,
     gacc, gbuf, cs, dt, dbank,
-    ms, mr, s1, v1, s2, v2, s3, v3, hs, hr, gs, gr, ds_, dr,
+    ms, mr, ts, tr, hs, hr, gs, gr, ds_, dr,
 ):
     slots, rows, cols = sci.shape
     taps = 31
     count = 31
-    half = rows // 2
+    chunk_rows = rows // CHUNKS
     nv, nq = lax.axis_size("visit"), lax.axis_size("quad")
     me, q = lax.axis_index("visit"), lax.axis_index("quad")
     blocks = cols // LANES
-    groups = half // 8
+    groups = chunk_rows // 8
 
     def at_visit(step):
         return lax.rem(me + step + nv, nv)
@@ -75,13 +76,6 @@
     for copy in meta_copies:
         copy.start()
     ahead = [{"visit": at_visit(sign)} for sign in SIGN]
-    hop1 = [
-        remote(tiles.at[t], t1.at[d, t], s1.at[d, t], v1.at[d, t], ahead[d])
-        for t in range(slots) for d in range(2)
-    ]
-    for copy in hop1:
-        copy.start()
-
     tst[...] = jnp.zeros_like(tst)
     bmat[...] = jnp.zeros_like(bmat)
     blank = jnp.zeros((32, LANES), F32)
@@ -102,15 +96,19 @@
         first = pl.multiple_of(k * rows, 16)
         line_k = jnp.broadcast_to(base[0, pl.ds(k, 1), :], (rows, 2 * LANES))
         rmat[pl.ds(first, rows), :] = pltpu.roll(line_k, 0, 1, stride=1, stride_axis=0).astype(BF16)
-        for part in range(2):
-            line_k = jnp.broadcast_to(base[1 + part, pl.ds(k, 1), :], (EXT, 2 * LANES))
-            band = pltpu.roll(line_k, 0, 1, stride=1, stride_axis=0)
-            for piece in range(2):
-                if piece:
-                    band = pltpu.roll(band, EXT, 1)
-                bmat[k, piece * EXT:(piece + 1) * EXT, part * LANES:(part + 1) * LANES] = (
-                    band[:, :LANES].astype(BF16)
-                )
+
+    def bands(first, last):
+        @pl.loop(first, last)
+        def _(k):
+            for part in range(2):
+                line_k = jnp.broadcast_to(base[1 + part, pl.ds(k, 1), :], (EXT, 2 * LANES))
+                band = pltpu.roll(line_k, 0, 1, stride=1, stride_axis=0)
+                for piece in range(2):
+                    if piece:
+                        band = pltpu.roll(band, EXT, 1)
+                    bmat[k, piece * EXT:(piece + 1) * EXT, part * LANES:(part + 1) * LANES] = (
+                        band[:, :LANES].astype(BF16)
+                    )
 
     @pl.when(q == 0)
     def _():
@@ -134,57 +132,27 @@
         return jnp.where(column >= wide(2), wide(0), wide(1))
 
     def group(part, g):
-        return pl.ds(part * half + g * 8, 8)
+        return pl.ds(part * chunk_rows + g * 8, 8)
 
     def part_rows(part):
-        return pl.ds(part * half, half)
-
-    for copy in hop1:
-        copy.wait_recv()
-
-    def second(d, slot, part):
-        return remote(snd2.at[d, slot, part_rows(part)], r2.at[d, slot, part_rows(part)],
-                      s2.at[d, slot, part], v2.at[d, slot, part], ahead[d])
-
-    def third(d, slot, part):
-        return remote(r2.at[d, slot, part_rows(part)], r3.at[d, slot, part_rows(part)],
-                      s3.at[d, slot, part], v3.at[d, slot, part], ahead[d])
-
-    def build(slot, part):
+        return pl.ds(part * chunk_rows, chunk_rows)
+
+    def hop_copy(d, hop, slot, part):
+        return remote(bank.at[hop - 1, d, slot, part_rows(part)], bank.at[hop, d, slot, part_rows(part)],
+                      ts.at[hop - 1, d, slot, part], tr.at[hop - 1, d, slot, part], ahead[d])
+
+    def relay(hop, slot, part):
         for d, sign in enumerate(SIGN):
-            wanted = owner(2 * sign, slot)
-            source = at_visit(-sign)
+            wanted = owner((REACH - hop) * sign, slot)
+            if hop:
+                hop_copy(d, hop, slot, part).wait_recv()
             for g in range(groups):
-                total = jnp.zeros((8, cols), F32)
+                sl = group(part, g)
+                total = bank[hop, d, slot, sl, :] if hop else jnp.zeros((8, cols), F32)
                 for t in range(slots):
-                    total = jnp.where(wanted == slots * me + t, tiles[t, group(part, g), :], total)
-                    total = jnp.where(wanted == slots * source + t, t1[d, t, group(part, g), :], total)
-                snd2[d, slot, group(part, g), :] = total
-
-    def start_second(slot, part):
-        for d in range(2):
-            second(d, slot, part).start()
-
-    def relay(slot, part):
-        for d, sign in enumerate(SIGN):
-            wanted = owner(sign, slot)
-            second(d, slot, part).wait_recv()
-            for g in range(groups):
-                total = r2[d, slot, group(part, g), :]
-                for t in range(slots):
-                    total = jnp.where(wanted == slots * me + t, tiles[t, group(part, g), :], total)
-                r2[d, slot, group(part, g), :] = total
-            third(d, slot, part).start()
-
-    for part in range(2):
-        build(0, part)
-        start_second(0, part)
-    for part in range(2):
-        build(1, part)
-    for part in range(2):
-        relay(0, part)
-    for part in range(2):
-        start_second(1, part)
+                    total = jnp.where(wanted == slots * me + t, tiles[t, sl, :], total)
+                bank[hop, d, slot, sl, :] = total
+            hop_copy(d, hop + 1, slot, part).start()
 
     def halo_copies(slot):
         down = remote(pre.at[slot, pl.ds(rows - HALO, HALO)], halo.at[slot, 0],
@@ -212,14 +180,21 @@
     own_row = lax.broadcasted_iota(jnp.int32, (32, LANES), 0)
     own_col = lax.broadcasted_iota(jnp.int32, (32, LANES), 1)
 
-    def convolve(slot, events):
-        for part in range(2):
+    def gram_copies(slot):
+        return [
+            remote(gbuf.at[slot, 0], gbuf.at[slot, step], gs.at[slot, step - 1], gr.at[slot, step - 1],
+                   {"quad": at_quad(step)})
+            for step in range(1, nq)
+        ]
+
+    def assemble(slot):
+        for part in range(CHUNKS):
             for d in range(2):
-                third(d, slot, part).wait_recv()
+                hop_copy(d, REACH, slot, part).wait_recv()
         wanted = owner(0, slot)
         for g in range(rows // 8):
             sl = pl.ds(g * 8, 8)
-            total = r3[0, slot, sl, :] + r3[1, slot, sl, :]
+            total = bank[REACH, 0, slot, sl, :] + bank[REACH, 1, slot, sl, :]
             for t in range(slots):
                 total = jnp.where(wanted == slots * me + t, tiles[t, sl, :], total)
             pre[slot, sl, :] = total
@@ -236,6 +211,9 @@
         for g in range(rows // HALO):
             spread(pre[slot, g * HALO:(g + 1) * HALO, :], slot, HALO + g * HALO)
 
+    def edges(slot):
+        down, up = halo_copies(slot)
+
         @pl.when(q > 0)
         def _():
             down.wait_recv()
@@ -246,11 +224,11 @@
 
         spread(halo[slot, 0], slot, 0)
         spread(halo[slot, 1], slot, HALO + rows)
-        events[0]()
-
+
+    def row_step():
         chunk = count * HALO
 
-        @pl.loop(0, (cols + 2 * LANES) // (2 * LANES))
+        @pl.loop(0, (cols + 2 * LANES) // (2 * LANES), unroll=True)
         def _(n):
             sl = pl.ds(pl.multiple_of(n * 2 * LANES, 2 * LANES), 2 * LANES)
             weight = tst[:, sl]
@@ -260,31 +238,31 @@
                 yhi[rsl, sl] = high
                 ylo[rsl, sl] = low
 
-        events[1]()
-        bounds = (0, 8, 16, 24, count)
-        for segment in range(4):
-            @pl.loop(bounds[segment], bounds[segment + 1])
-            def _(k):
-                rsl = pl.ds(pl.multiple_of(k * rows, 16), rows)
-                left = jnp.concatenate(
-                    [y[rsl, n * LANES:(n + 2) * LANES] for y in (yhi, ylo) for n in range(blocks)], axis=0
-                )
-                out = jnp.dot(left, bmat[k], preferred_element_type=F32)
-                out = out[:, :LANES] + out[:, LANES:]
-                out = out[:rows * blocks] + out[rows * blocks:]
-                for n in range(blocks):
-                    img[k, :, n * LANES:(n + 1) * LANES] = out[n * rows:(n + 1) * rows]
-            events[2 + segment]()
-
+    bounds = (0, 8, 16, 24, count)
+
+    def column_step(segment):
+        @pl.loop(bounds[segment], bounds[segment + 1], unroll=True)
+        def _(k):
+            rsl = pl.ds(pl.multiple_of(k * rows, 16), rows)
+            left = jnp.concatenate(
+                [y[rsl, n * LANES:(n + 2) * LANES] for y in (yhi, ylo) for n in range(blocks)], axis=0
+            )
+            out = jnp.dot(left, bmat[k], preferred_element_type=F32)
+            out = out[:, :LANES] + out[:, LANES:]
+            out = out[:rows * blocks] + out[rows * blocks:]
+            for n in range(blocks):
+                img[k, :, n * LANES:(n + 1) * LANES] = out[n * rows:(n + 1) * rows]
+
+    def products(slot):
         img[count] = sci[slot]
         gacc[...] = jnp.zeros_like(gacc)
 
-        @pl.loop(0, rows // 8)
+        @pl.loop(0, rows // 8, unroll=True)
         def _(g):
             x = img[:, pl.ds(pl.multiple_of(g * 8, 8), 8), :].reshape(256, cols)
             high, low = split(x)
-            both = jnp.concatenate([high, low], axis=0)
-            gacc[...] += lax.dot_general(high, both, (((1,), (1,)), ((), ())), preferred_element_type=F32)
+            gacc[:, :256] += lax.dot_general(high, high, (((1,), (1,)), ((), ())), preferred_element_type=F32)
+            gacc[:, 256:] += lax.dot_general(high, low, (((1,), (1,)), ((), ())), preferred_element_type=F32)
 
         srow = lax.broadcasted_iota(jnp.int32, (256, 256), 0)
         scol = lax.broadcasted_iota(jnp.int32, (256, 256), 1)
@@ -301,21 +279,19 @@
         cross = reduced(gacc[:, 256:])
         square = jnp.concatenate([cross, jnp.zeros((96, LANES), F32)], axis=0)
         gbuf[slot, 0] = main + cross + square.T[:32]
-        copies = [
-            remote(gbuf.at[slot, 0], gbuf.at[slot, step], gs.at[slot, step - 1], gr.at[slot, step - 1],
-                   {"quad": at_quad(step)})
-            for step in range(1, nq)
-        ]
-        for copy in copies:
+        for copy in gram_copies(slot):
             copy.start()
-        events[6]()
-        for copy in copies:
+
+    def solve(slot, middle):
+        for copy in gram_copies(slot):
             copy.wait_recv()
         total = gbuf[slot, lax.rem(q + nq, nq)]
         for source in range(1, nq):
             total = total + gbuf[slot, lax.rem(q + nq - source, nq)]
         system = total / pixels + jnp.where((own_row == own_col) & (own_col < count), 0.01, 0.0)
         for j in range(count):
+            if j == count // 2:
+                middle()
             pivot_row = system[j:j + 1, :]
             pivot_col = jnp.broadcast_to(system[:, j:j + 1], (32, LANES))
             pivot = jnp.broadcast_to(system[j:j + 1, j:j + 1], (1, LANES))
@@ -323,7 +299,8 @@
             system = jnp.where(own_row == j, scaled, system - pivot_col * scaled)
         cs[...] = jnp.broadcast_to(system[:, count:count + 1], (32, LANES))
 
-        @pl.loop(0, rows // 8)
+    def subtract(slot):
+        @pl.loop(0, rows // 8, unroll=True)
         def _(g):
             sl = pl.ds(pl.multiple_of(g * 8, 8), 8)
             total = sci[slot, sl, :]
@@ -339,7 +316,7 @@
                       ds_.at[d, hop, slot, part], dr.at[d, hop, slot, part], ahead[d])
 
     def start_spread(slot):
-        for part in range(2):
+        for part in range(CHUNKS):
             for d in range(2):
                 spread_copy(d, 0, slot, part).start()
 
@@ -349,7 +326,7 @@
             if hop + 1 < REACH:
                 spread_copy(d, hop + 1, slot, part).start()
 
-    def add(step, slot, data, parts=(0, 1)):
+    def add(step, slot, data, parts=range(CHUNKS)):
         wanted = owner(step, slot)
         for part in parts:
             for g in range(groups):
@@ -360,44 +337,76 @@
     def nothing():
         pass
 
-    relay_events = [nothing] * 7
-    relay_events[1] = functools.partial(relay, 1, 0)
-    relay_events[2] = functools.partial(relay, 1, 1)
-    convolve(0, relay_events)
-    start_spread(0)
+    for part in range(CHUNKS):
+        relay(0, 0, part)
+    bands(0, 16)
+    for part in range(CHUNKS):
+        relay(1, 0, part)
+    bands(16, 24)
+    for part in range(CHUNKS):
+        relay(2, 0, part)
+    for part in range(CHUNKS):
+        relay(0, 1, part)
+    bands(24, count)
     for t in range(slots):
         coadd[t] = jnp.zeros((rows, cols), F32)
+
+    assemble(0)
+    relay(1, 1, 0)
+    relay(1, 1, 1)
+    edges(0)
+    row_step()
+    relay(1, 1, 2)
+    column_step(0)
+    relay(2, 1, 0)
+    column_step(1)
+    relay(2, 1, 1)
+    column_step(2)
+    relay(2, 1, 2)
+    column_step(3)
+    products(0)
+    assemble(1)
+    solve(0, nothing)
+    subtract(0)
+    start_spread(0)
+
+    edges(1)
+    row_step()
+    column_step(0)
+    column_step(1)
+    column_step(2)
+    forward(0, 0, 0)
+    column_step(3)
+    forward(0, 0, 1)
+    products(1)
     add(0, 0, dt.at[0])
-
-    spread_events = [nothing] * 7
-    spread_events[1] = functools.partial(forward, 0, 0, 0)
-    spread_events[2] = functools.partial(forward, 0, 0, 1)
-    spread_events[3] = functools.partial(forward, 1, 0, 0)
-    spread_events[4] = functools.partial(forward, 1, 0, 1)
-    convolve(1, spread_events)
+    forward(0, 0, 2)
+    forward(1, 0, 0)
+    forward(1, 0, 1)
+    solve(1, functools.partial(forward, 1, 0, 2))
+    subtract(1)
     start_spread(1)
+
     add(0, 1, dt.at[1])
     for d, sign in enumerate(SIGN):
         add(-sign, 0, dbank.at[d, 0, 0])
-    forward(0, 1, 0)
-    forward(0, 1, 1)
+    for part in range(CHUNKS):
+        forward(0, 1, part)
     for d, sign in enumerate(SIGN):
         add(-2 * sign, 0, dbank.at[d, 1, 0])
-    forward(1, 1, 0)
-    forward(1, 1, 1)
-    forward(2, 0, 0)
-    forward(2, 0, 1)
+    for part in range(CHUNKS):
+        forward(1, 1, part)
+    for part in range(CHUNKS):
+        forward(2, 0, part)
     for d, sign in enumerate(SIGN):
         add(-3 * sign, 0, dbank.at[d, 2, 0])
         add(-sign, 1, dbank.at[d, 0, 1])
         add(-2 * sign, 1, dbank.at[d, 1, 1])
-    for part in range(2):
+    for part in range(CHUNKS):
         forward(2, 1, part)
         for d, sign in enumerate(SIGN):
             add(-3 * sign, 1, dbank.at[d, 2, 1], (part,))
 
-    for copy in hop1:
-        copy.wait_send()
     for slot in range(slots):
         down, up = halo_copies(slot)
 
@@ -409,14 +418,12 @@
         def _():
             up.wait_send()
 
-        for step in range(1, nq):
-            remote(gbuf.at[slot, 0], gbuf.at[slot, step], gs.at[slot, step - 1], gr.at[slot, step - 1],
-                   {"quad": at_quad(step)}).wait_send()
-        for part in range(2):
+        for copy in gram_copies(slot):
+            copy.wait_send()
+        for part in range(CHUNKS):
             for d in range(2):
-                second(d, slot, part).wait_send()
-                third(d, slot, part).wait_send()
                 for hop in range(REACH):
+                    hop_copy(d, hop + 1, slot, part).wait_send()
                     spread_copy(d, hop, slot, part).wait_send()
 
 
@@ -439,10 +446,7 @@
         out_specs=[vmem, vmem],
         scratch_shapes=[
             pltpu.VMEM((2 * REACH + 1, 8, LANES), jnp.int32),
-            pltpu.VMEM((2, slots, rows, cols), F32),
-            pltpu.VMEM((2, slots, rows, cols), F32),
-            pltpu.VMEM((2, slots, rows, cols), F32),
-            pltpu.VMEM((2, slots, rows, cols), F32),
+            pltpu.VMEM((REACH + 1, 2, slots, rows, cols), F32),
             pltpu.VMEM((slots, rows, cols), F32),
             pltpu.VMEM((slots, 2, HALO, cols), F32),
             pltpu.VMEM((256, ext_cols), BF16),
@@ -458,12 +462,10 @@
             pltpu.VMEM((slots, rows, cols), F32),
             pltpu.VMEM((2, REACH, slots, rows, cols), F32),
             dma((2 * REACH + 1,)), dma((2 * REACH + 1,)),
-            dma((2, slots)), dma((2, slots)),
-            dma((2, slots, 2)), dma((2, slots, 2)),
-            dma((2, slots, 2)), dma((2, slots, 2)),
+            dma((REACH, 2, slots, CHUNKS)), dma((REACH, 2, slots, CHUNKS)),
             dma((slots, 2)), dma((slots, 2)),
             dma((slots, nq - 1)), dma((slots, nq - 1)),
-            dma((2, REACH, slots, 2)), dma((2, REACH, slots, 2)),
+            dma((2, REACH, slots, CHUNKS)), dma((2, REACH, slots, CHUNKS)),
         ],
         compiler_params=pltpu.CompilerParams(
             collective_id=0, has_side_effects=True, vmem_limit_bytes=56 * 1024 * 1024

time: 136 us -> 119 us (0.88)
  Pallas kernels: 130 us -> 114 us
    pallas_call x1, Pallas kernels: 130 us -> 114 us  [on_device(): pl.pallas_call(functools.partial(kernel, float(pixels)), out_shape=[jax.S...]
where the time goes in v2:
time: 119 us
  Pallas kernels  114 us (96%)
  local copies, waits for them, and re-layouts  4.59 us (4%)
    pallas_call x1, Pallas kernels, on_device(): pl.pallas_call(functools.partial(kernel, float(pixels)), out_shape=[jax.S...  114 us
    unnamed x6, local copies, waits for them, and re-layouts  2.57 us

profile of v2, /device:TPU:1, one launch (start us, length us, event | category | flops | bytes accessed | tf_op | source)
XLA Modules:
  0.0 118.9 jit_solution(8140180435914043800)
XLA Ops:
  0.6 0.0 copy-start.1
  0.6 1.3 %pad.7.brow = f32[32,128]{1,0:T(8,128)} pad(f32[31,31]{1,0:T(8,128)} %param.10, f32[]{:T(128)} %constant.2.clone.1), padding=0_1x0_97 | pad | bytes 20232 | tf_op jit(solution)/shard_map/jit(_pad)/pad | solution.py:436
  2.0 0.0 copy-done.1
  2.0 0.1 rev.3
  2.0 0.6 pad.8.bcol
  2.7 113.7 %shard_map.77 = (f32[2,48,1024]{2,1,0:T(8,128)}, f32[2,48,1024]{2,1,0:T(8,128)}) custom-call(f32[2,48,1024]{2,1,0:T(8,128)} %sci.1, f32[2,48,1024]{2,1,0:T(8,128)} %tiles.1, s32[2,2]{1,0:T(2,128)} %pairs.1, s32[2]{0:T(128)} %offs.1, f32[32,128]{1,0:T(8,128)} %pad.7.brow, f32[32,128]{1,0:T(8,128)} %pad.8.bcol), custom_call_target="tpu_custom_call" | custom-call | flops 8000000000 | bytes 2000000 | tf_op jit(solution)/shard_map/pallas_call | solution.py:442
  116.3 0.0 copy-start
  116.3 1.8 %copy.10 = f32[2,48,1024]{2,1,0:T(8,128)} copy(f32[2,48,1024]{2,1,0:T(8,128)} %get-tuple-element.4) | data formatting | bytes 786432
  118.2 0.0 copy-done
  118.2 0.7 copy.11
Async XLA Ops:
  0.6 1.3 %copy-start.1 = (f32[31,31]{1,0:T(8,128)S(1)}, f32[31,31]{1,0:T(8,128)}, u32[]{:S(2)}) copy-start(f32[31,31]{1,0:T(8,128)} %param.11) | copy-start | bytes 11536
  116.3 1.8 %copy-start = (f32[2,48,1024]{2,1,0:T(8,128)S(1)}, f32[2,48,1024]{2,1,0:T(8,128)}, u32[]{:S(2)}) copy-start(f32[2,48,1024]{2,1,0:T(8,128)} %get-tuple-element.5) | copy-start | bytes 1179652

commit v3 on v2

--- a/solution.py
+++ b/solution.py
@@ -289,34 +289,40 @@
         for source in range(1, nq):
             total = total + gbuf[slot, lax.rem(q + nq - source, nq)]
         system = total / pixels + jnp.where((own_row == own_col) & (own_col < count), 0.01, 0.0)
-        for j in range(count):
-            if j == count // 2:
+        for j in range(0, count - 1, 2):
+            if j == count // 2 - 1:
                 middle()
-            pivot_row = system[j:j + 1, :]
-            pivot_col = jnp.broadcast_to(system[:, j:j + 1], (32, LANES))
-            pivot = jnp.broadcast_to(system[j:j + 1, j:j + 1], (1, LANES))
-            scaled = pivot_row * (1.0 / pivot)
-            system = jnp.where(own_row == j, scaled, system - pivot_col * scaled)
+            first_col = jnp.broadcast_to(system[:, j:j + 1], (32, LANES))
+            second_col = jnp.broadcast_to(system[:, j + 1:j + 2], (32, LANES))
+            first_row, second_row = system[j:j + 1, :], system[j + 1:j + 2, :]
+            a, b = first_col[j:j + 1, :], second_col[j:j + 1, :]
+            c, d = first_col[j + 1:j + 2, :], second_col[j + 1:j + 2, :]
+            inverse = 1.0 / (a * d - b * c)
+            first = (d * first_row - b * second_row) * inverse
+            second = (a * second_row - c * first_row) * inverse
+            rest = system - first_col * first - second_col * second
+            system = jnp.where(own_row == j, first, jnp.where(own_row == j + 1, second, rest))
+        last = count - 1
+        pivot_col = jnp.broadcast_to(system[:, last:last + 1], (32, LANES))
+        scaled = system[last:last + 1, :] * (1.0 / pivot_col[last:last + 1, :])
+        system = jnp.where(own_row == last, scaled, system - pivot_col * scaled)
         cs[...] = jnp.broadcast_to(system[:, count:count + 1], (32, LANES))
-
-    def subtract(slot):
-        @pl.loop(0, rows // 8, unroll=True)
-        def _(g):
-            sl = pl.ds(pl.multiple_of(g * 8, 8), 8)
-            total = sci[slot, sl, :]
-            for k in range(count):
-                weight = jnp.broadcast_to(cs[k:k + 1, :], (8, LANES))
-                total = total - jnp.concatenate([weight] * blocks, axis=1) * img[k, sl, :]
-            diff[slot, sl, :] = total
-            dt[slot, sl, :] = pltpu.roll(total, offs[slot], 1)
 
     def spread_copy(d, hop, slot, part):
         source = dt.at[slot, part_rows(part)] if hop == 0 else dbank.at[d, hop - 1, slot, part_rows(part)]
         return remote(source, dbank.at[d, hop, slot, part_rows(part)],
                       ds_.at[d, hop, slot, part], dr.at[d, hop, slot, part], ahead[d])
 
-    def start_spread(slot):
+    def subtract(slot):
         for part in range(CHUNKS):
+            for g in range(groups):
+                sl = group(part, g)
+                total = sci[slot, sl, :]
+                for k in range(count):
+                    weight = jnp.broadcast_to(cs[k:k + 1, :], (8, LANES))
+                    total = total - jnp.concatenate([weight] * blocks, axis=1) * img[k, sl, :]
+                diff[slot, sl, :] = total
+                dt[slot, sl, :] = pltpu.roll(total, offs[slot], 1)
             for d in range(2):
                 spread_copy(d, 0, slot, part).start()
 
@@ -358,17 +364,17 @@
     row_step()
     relay(1, 1, 2)
     column_step(0)
+    column_step(1)
     relay(2, 1, 0)
-    column_step(1)
+    column_step(2)
     relay(2, 1, 1)
-    column_step(2)
-    relay(2, 1, 2)
     column_step(3)
     products(0)
-    assemble(1)
+    relay(2, 1, 2)
     solve(0, nothing)
     subtract(0)
-    start_spread(0)
+    assemble(1)
+    add(0, 0, dt.at[0])
 
     edges(1)
     row_step()
@@ -379,13 +385,11 @@
     column_step(3)
     forward(0, 0, 1)
     products(1)
-    add(0, 0, dt.at[0])
     forward(0, 0, 2)
     forward(1, 0, 0)
     forward(1, 0, 1)
     solve(1, functools.partial(forward, 1, 0, 2))
     subtract(1)
-    start_spread(1)
 
     add(0, 1, dt.at[1])
     for d, sign in enumerate(SIGN):

time: 119 us -> 114 us (0.958)
  the two profiles are of different devices: /device:TPU:1 before, /device:TPU:3 now
where the time goes in v3:
time: 114 us
  Pallas kernels  108 us (95%)
  local copies, waits for them, and re-layouts  4.59 us (4%)
    pallas_call x1, Pallas kernels, on_device(): pl.pallas_call(functools.partial(kernel, float(pixels)), out_shape=[jax.S...  108 us
    unnamed x6, local copies, waits for them, and re-layouts  2.57 us

profile of v3, /device:TPU:3, one launch (start us, length us, event | category | flops | bytes accessed | tf_op | source)
XLA Modules:
  0.0 113.7 jit_solution(3570692284005462555)
XLA Ops:
  0.6 0.0 copy-start.1
  0.6 1.3 %pad.7.brow = f32[32,128]{1,0:T(8,128)} pad(f32[31,31]{1,0:T(8,128)} %param.10, f32[]{:T(128)} %constant.2.clone.1), padding=0_1x0_97 | pad | bytes 20232 | tf_op jit(solution)/shard_map/jit(_pad)/pad | solution.py:440
  2.0 0.0 copy-done.1
  2.0 0.1 rev.3
  2.0 0.6 pad.8.bcol
  2.7 108.4 %shard_map.77 = (f32[2,48,1024]{2,1,0:T(8,128)}, f32[2,48,1024]{2,1,0:T(8,128)}) custom-call(f32[2,48,1024]{2,1,0:T(8,128)} %sci.1, f32[2,48,1024]{2,1,0:T(8,128)} %tiles.1, s32[2,2]{1,0:T(2,128)} %pairs.1, s32[2]{0:T(128)} %offs.1, f32[32,128]{1,0:T(8,128)} %pad.7.brow, f32[32,128]{1,0:T(8,128)} %pad.8.bcol), custom_call_target="tpu_custom_call" | custom-call | flops 8000000000 | bytes 2000000 | tf_op jit(solution)/shard_map/pallas_call | solution.py:446
  111.1 0.0 copy-start
  111.1 1.8 %copy.10 = f32[2,48,1024]{2,1,0:T(8,128)} copy(f32[2,48,1024]{2,1,0:T(8,128)} %get-tuple-element.4) | data formatting | bytes 786432
  112.9 0.0 copy-done
  112.9 0.7 copy.11
Async XLA Ops:
  0.6 1.3 %copy-start.1 = (f32[31,31]{1,0:T(8,128)S(1)}, f32[31,31]{1,0:T(8,128)}, u32[]{:S(2)}) copy-start(f32[31,31]{1,0:T(8,128)} %param.11) | copy-start | bytes 11536
  111.1 1.8 %copy-start = (f32[2,48,1024]{2,1,0:T(8,128)S(1)}, f32[2,48,1024]{2,1,0:T(8,128)}, u32[]{:S(2)}) copy-start(f32[2,48,1024]{2,1,0:T(8,128)} %get-tuple-element.5) | copy-start | bytes 1179652

commit v4 on v3

--- a/solution.py
+++ b/solution.py
@@ -93,9 +93,11 @@
 
     @pl.loop(0, count)
     def _(k):
-        first = pl.multiple_of(k * rows, 16)
         line_k = jnp.broadcast_to(base[0, pl.ds(k, 1), :], (rows, 2 * LANES))
-        rmat[pl.ds(first, rows), :] = pltpu.roll(line_k, 0, 1, stride=1, stride_axis=0).astype(BF16)
+        line_k = pltpu.roll(line_k, 0, 1, stride=1, stride_axis=0).astype(BF16)
+        for part in range(CHUNKS):
+            first = pl.multiple_of(part * count * chunk_rows + k * chunk_rows, 16)
+            rmat[pl.ds(first, chunk_rows), :] = line_k[part * chunk_rows:(part + 1) * chunk_rows]
 
     def bands(first, last):
         @pl.loop(first, last)
@@ -191,6 +193,8 @@
         for part in range(CHUNKS):
             for d in range(2):
                 hop_copy(d, REACH, slot, part).wait_recv()
+        img[count] = sci[slot]
+        gacc[...] = jnp.zeros_like(gacc)
         wanted = owner(0, slot)
         for g in range(rows // 8):
             sl = pl.ds(g * 8, 8)
@@ -225,45 +229,48 @@
         spread(halo[slot, 0], slot, 0)
         spread(halo[slot, 1], slot, HALO + rows)
 
-    def row_step():
-        chunk = count * HALO
+    def row_step(parts):
+        chunk = count * chunk_rows
 
         @pl.loop(0, (cols + 2 * LANES) // (2 * LANES), unroll=True)
         def _(n):
             sl = pl.ds(pl.multiple_of(n * 2 * LANES, 2 * LANES), 2 * LANES)
             weight = tst[:, sl]
-            for piece in range(count * rows // chunk):
-                rsl = pl.ds(piece * chunk, chunk)
+            for part in parts:
+                rsl = pl.ds(part * chunk, chunk)
                 high, low = split(jnp.dot(rmat[rsl, :], weight, preferred_element_type=F32))
                 yhi[rsl, sl] = high
                 ylo[rsl, sl] = low
 
-    bounds = (0, 8, 16, 24, count)
-
-    def column_step(segment):
-        @pl.loop(bounds[segment], bounds[segment + 1], unroll=True)
+    def column_step(begin, end, parts):
+        @pl.loop(begin, end, unroll=True)
         def _(k):
-            rsl = pl.ds(pl.multiple_of(k * rows, 16), rows)
-            left = jnp.concatenate(
-                [y[rsl, n * LANES:(n + 2) * LANES] for y in (yhi, ylo) for n in range(blocks)], axis=0
-            )
-            out = jnp.dot(left, bmat[k], preferred_element_type=F32)
+            left = []
+            for y in (yhi, ylo):
+                for part in parts:
+                    first = pl.multiple_of(part * count * chunk_rows + k * chunk_rows, 16)
+                    for n in range(blocks):
+                        left.append(y[pl.ds(first, chunk_rows), n * LANES:(n + 2) * LANES])
+            out = jnp.dot(jnp.concatenate(left, axis=0), bmat[k], preferred_element_type=F32)
             out = out[:, :LANES] + out[:, LANES:]
-            out = out[:rows * blocks] + out[rows * blocks:]
-            for n in range(blocks):
-                img[k, :, n * LANES:(n + 1) * LANES] = out[n * rows:(n + 1) * rows]
-
-    def products(slot):
-        img[count] = sci[slot]
-        gacc[...] = jnp.zeros_like(gacc)
-
-        @pl.loop(0, rows // 8, unroll=True)
-        def _(g):
-            x = img[:, pl.ds(pl.multiple_of(g * 8, 8), 8), :].reshape(256, cols)
-            high, low = split(x)
-            gacc[:, :256] += lax.dot_general(high, high, (((1,), (1,)), ((), ())), preferred_element_type=F32)
-            gacc[:, 256:] += lax.dot_general(high, low, (((1,), (1,)), ((), ())), preferred_element_type=F32)
-
+            size = len(parts) * blocks * chunk_rows
+            out = out[:size] + out[size:]
+            for place, part in enumerate(parts):
+                for n in range(blocks):
+                    first = (place * blocks + n) * chunk_rows
+                    img[k, part * chunk_rows:(part + 1) * chunk_rows, n * LANES:(n + 1) * LANES] = (
+                        out[first:first + chunk_rows]
+                    )
+
+    def products(slot, parts):
+        for part in parts:
+            for g in range(groups):
+                x = img[:, part * chunk_rows + g * 8:part * chunk_rows + (g + 1) * 8, :].reshape(256, cols)
+                high, low = split(x)
+                gacc[:, :256] += lax.dot_general(high, high, (((1,), (1,)), ((), ())), preferred_element_type=F32)
+                gacc[:, 256:] += lax.dot_general(high, low, (((1,), (1,)), ((), ())), preferred_element_type=F32)
+
+    def send_products(slot):
         srow = lax.broadcasted_iota(jnp.int32, (256, 256), 0)
         scol = lax.broadcasted_iota(jnp.int32, (256, 256), 1)
         same = lax.rem(srow, 8) == lax.rem(scol, 8)
@@ -357,35 +364,40 @@
     for t in range(slots):
         coadd[t] = jnp.zeros((rows, cols), F32)
 
+    inner, outer = (1,), (0, 2)
     assemble(0)
     relay(1, 1, 0)
+    row_step(inner)
     relay(1, 1, 1)
+    column_step(0, count, inner)
+    relay(1, 1, 2)
+    products(0, inner)
     edges(0)
-    row_step()
-    relay(1, 1, 2)
-    column_step(0)
-    column_step(1)
+    row_step(outer)
+    column_step(0, 16, outer)
     relay(2, 1, 0)
-    column_step(2)
+    column_step(16, count, outer)
     relay(2, 1, 1)
-    column_step(3)
-    products(0)
+    products(0, outer)
+    send_products(0)
     relay(2, 1, 2)
     solve(0, nothing)
     subtract(0)
+
     assemble(1)
+    row_step(inner)
+    column_step(0, count, inner)
+    products(1, inner)
+    edges(1)
+    row_step(outer)
+    forward(0, 0, 0)
+    column_step(0, 16, outer)
+    forward(0, 0, 1)
+    column_step(16, count, outer)
+    forward(0, 0, 2)
+    products(1, outer)
+    send_products(1)
     add(0, 0, dt.at[0])
-
-    edges(1)
-    row_step()
-    column_step(0)
-    column_step(1)
-    column_step(2)
-    forward(0, 0, 0)
-    column_step(3)
-    forward(0, 0, 1)
-    products(1)
-    forward(0, 0, 2)
     forward(1, 0, 0)
     forward(1, 0, 1)
     solve(1, functools.partial(forward, 1, 0, 2))

time: 114 us -> 117 us (1.026)
  Pallas kernels: 108 us -> 111 us
    pallas_call x1, Pallas kernels: 108 us -> 111 us  [on_device(): pl.pallas_call(functools.partial(kernel, float(pixels)), out_shape=[jax.S...]
where the time goes in v4:
time: 117 us; the launch traced here: 116 us
  Pallas kernels  111 us (95%)
  local copies, waits for them, and re-layouts  4.59 us (4%)
    pallas_call x1, Pallas kernels, on_device(): pl.pallas_call(functools.partial(kernel, float(pixels)), out_shape=[jax.S...  111 us
    unnamed x6, local copies, waits for them, and re-layouts  2.57 us

profile of v4, /device:TPU:3, one launch (start us, length us, event | category | flops | bytes accessed | tf_op | source)
XLA Modules:
  0.0 116.5 jit_solution(1498975532942241262)
XLA Ops:
  0.6 0.0 copy-start.1
  0.6 1.3 %pad.7.brow = f32[32,128]{1,0:T(8,128)} pad(f32[31,31]{1,0:T(8,128)} %param.10, f32[]{:T(128)} %constant.2.clone.1), padding=0_1x0_97 | pad | bytes 20232 | tf_op jit(solution)/shard_map/jit(_pad)/pad | solution.py:452
  2.0 0.0 copy-done.1
  2.0 0.1 rev.3
  2.0 0.6 pad.8.bcol
  2.7 111.2 %shard_map.77 = (f32[2,48,1024]{2,1,0:T(8,128)}, f32[2,48,1024]{2,1,0:T(8,128)}) custom-call(f32[2,48,1024]{2,1,0:T(8,128)} %sci.1, f32[2,48,1024]{2,1,0:T(8,128)} %tiles.1, s32[2,2]{1,0:T(2,128)} %pairs.1, s32[2]{0:T(128)} %offs.1, f32[32,128]{1,0:T(8,128)} %pad.7.brow, f32[32,128]{1,0:T(8,128)} %pad.8.bcol), custom_call_target="tpu_custom_call" | custom-call | flops 8000000000 | bytes 2000000 | tf_op jit(solution)/shard_map/pallas_call | solution.py:458
  113.9 0.0 copy-start
  113.9 1.8 %copy.10 = f32[2,48,1024]{2,1,0:T(8,128)} copy(f32[2,48,1024]{2,1,0:T(8,128)} %get-tuple-element.4) | data formatting | bytes 786432
  115.7 0.0 copy-done
  115.7 0.7 copy.11
Async XLA Ops:
  0.6 1.3 %copy-start.1 = (f32[31,31]{1,0:T(8,128)S(1)}, f32[31,31]{1,0:T(8,128)}, u32[]{:S(2)}) copy-start(f32[31,31]{1,0:T(8,128)} %param.11) | copy-start | bytes 11536
  113.9 1.8 %copy-start = (f32[2,48,1024]{2,1,0:T(8,128)S(1)}, f32[2,48,1024]{2,1,0:T(8,128)}, u32[]{:S(2)}) copy-start(f32[2,48,1024]{2,1,0:T(8,128)} %get-tuple-element.5) | copy-start | bytes 1179652

commit v5 on v3

--- a/solution.py
+++ b/solution.py
@@ -11,7 +11,7 @@
 REACH = 3
 LANES = 128
 HALO = 16
-CHUNKS = 3
+CHUNKS = 6
 EXT = 80
 HIGHEST = lax.Precision.HIGHEST
 F32 = jnp.float32
@@ -357,20 +357,24 @@
     for t in range(slots):
         coadd[t] = jnp.zeros((rows, cols), F32)
 
+    def third(step, hop, slot, place):
+        for part in range(place * CHUNKS // 3, (place + 1) * CHUNKS // 3):
+            step(hop, slot, part)
+
     assemble(0)
-    relay(1, 1, 0)
-    relay(1, 1, 1)
+    third(relay, 1, 1, 0)
+    third(relay, 1, 1, 1)
     edges(0)
     row_step()
-    relay(1, 1, 2)
+    third(relay, 1, 1, 2)
     column_step(0)
     column_step(1)
-    relay(2, 1, 0)
+    third(relay, 2, 1, 0)
     column_step(2)
-    relay(2, 1, 1)
+    third(relay, 2, 1, 1)
     column_step(3)
     products(0)
-    relay(2, 1, 2)
+    third(relay, 2, 1, 2)
     solve(0, nothing)
     subtract(0)
     assemble(1)
@@ -381,14 +385,14 @@
     column_step(0)
     column_step(1)
     column_step(2)
-    forward(0, 0, 0)
+    third(forward, 0, 0, 0)
     column_step(3)
-    forward(0, 0, 1)
+    third(forward, 0, 0, 1)
     products(1)
-    forward(0, 0, 2)
-    forward(1, 0, 0)
-    forward(1, 0, 1)
-    solve(1, functools.partial(forward, 1, 0, 2))
+    third(forward, 0, 0, 2)
+    third(forward, 1, 0, 0)
+    third(forward, 1, 0, 1)
+    solve(1, functools.partial(third, forward, 1, 0, 2))
     subtract(1)
 
     add(0, 1, dt.at[1])

time: 114 us -> 117 us (1.026)
  the two profiles are of different devices: /device:TPU:3 before, /device:TPU:1 now
where the time goes in v5:
time: 117 us; the launch traced here: 116 us
  Pallas kernels  111 us (95%)
  local copies, waits for them, and re-layouts  4.59 us (4%)
    pallas_call x1, Pallas kernels, on_device(): pl.pallas_call(functools.partial(kernel, float(pixels)), out_shape=[jax.S...  111 us
    unnamed x6, local copies, waits for them, and re-layouts  2.57 us

profile of v5, /device:TPU:1, one launch (start us, length us, event | category | flops | bytes accessed | tf_op | source)
XLA Modules:
  0.0 116.3 jit_solution(17614618967753035306)
XLA Ops:
  0.6 0.0 copy-start.1
  0.6 1.3 %pad.7.brow = f32[32,128]{1,0:T(8,128)} pad(f32[31,31]{1,0:T(8,128)} %param.10, f32[]{:T(128)} %constant.2.clone.1), padding=0_1x0_97 | pad | bytes 20232 | tf_op jit(solution)/shard_map/jit(_pad)/pad | solution.py:444
  2.0 0.0 copy-done.1
  2.0 0.1 rev.3
  2.0 0.6 pad.8.bcol
  2.7 111.0 %shard_map.77 = (f32[2,48,1024]{2,1,0:T(8,128)}, f32[2,48,1024]{2,1,0:T(8,128)}) custom-call(f32[2,48,1024]{2,1,0:T(8,128)} %sci.1, f32[2,48,1024]{2,1,0:T(8,128)} %tiles.1, s32[2,2]{1,0:T(2,128)} %pairs.1, s32[2]{0:T(128)} %offs.1, f32[32,128]{1,0:T(8,128)} %pad.7.brow, f32[32,128]{1,0:T(8,128)} %pad.8.bcol), custom_call_target="tpu_custom_call" | custom-call | flops 8000000000 | bytes 2000000 | tf_op jit(solution)/shard_map/pallas_call | solution.py:450
  113.7 0.0 copy-start
  113.7 1.8 %copy.10 = f32[2,48,1024]{2,1,0:T(8,128)} copy(f32[2,48,1024]{2,1,0:T(8,128)} %get-tuple-element.4) | data formatting | bytes 786432
  115.5 0.0 copy-done
  115.5 0.7 copy.11
Async XLA Ops:
  0.6 1.3 %copy-start.1 = (f32[31,31]{1,0:T(8,128)S(1)}, f32[31,31]{1,0:T(8,128)}, u32[]{:S(2)}) copy-start(f32[31,31]{1,0:T(8,128)} %param.11) | copy-start | bytes 11536
  113.7 1.8 %copy-start = (f32[2,48,1024]{2,1,0:T(8,128)S(1)}, f32[2,48,1024]{2,1,0:T(8,128)}, u32[]{:S(2)}) copy-start(f32[2,48,1024]{2,1,0:T(8,128)} %get-tuple-element.5) | copy-start | bytes 1179652

commit v6 on v3

--- a/solution.py
+++ b/solution.py
@@ -348,17 +348,18 @@
     bands(0, 16)
     for part in range(CHUNKS):
         relay(1, 0, part)
+    relay(0, 1, 0)
     bands(16, 24)
     for part in range(CHUNKS):
         relay(2, 0, part)
-    for part in range(CHUNKS):
+    for part in range(1, CHUNKS):
         relay(0, 1, part)
     bands(24, count)
     for t in range(slots):
         coadd[t] = jnp.zeros((rows, cols), F32)
 
+    relay(1, 1, 0)
     assemble(0)
-    relay(1, 1, 0)
     relay(1, 1, 1)
     edges(0)
     row_step()

time: 114 us -> 115 us (level)
  the two profiles are of different devices: /device:TPU:3 before, /device:TPU:1 now
where the time goes in v6:
time: 115 us
  Pallas kernels  110 us (96%)
  local copies, waits for them, and re-layouts  4.59 us (4%)
    pallas_call x1, Pallas kernels, on_device(): pl.pallas_call(functools.partial(kernel, float(pixels)), out_shape=[jax.S...  110 us
    unnamed x6, local copies, waits for them, and re-layouts  2.57 us

profile of v6, /device:TPU:1, one launch (start us, length us, event | category | flops | bytes accessed | tf_op | source)
XLA Modules:
  0.0 114.8 jit_solution(10825142894580286669)
XLA Ops:
  0.6 0.0 copy-start.1
  0.6 1.3 %pad.7.brow = f32[32,128]{1,0:T(8,128)} pad(f32[31,31]{1,0:T(8,128)} %param.10, f32[]{:T(128)} %constant.2.clone.1), padding=0_1x0_97 | pad | bytes 20232 | tf_op jit(solution)/shard_map/jit(_pad)/pad | solution.py:441
  2.0 0.0 copy-done.1
  2.0 0.1 rev.3
  2.0 0.6 pad.8.bcol
  2.7 109.5 %shard_map.77 = (f32[2,48,1024]{2,1,0:T(8,128)}, f32[2,48,1024]{2,1,0:T(8,128)}) custom-call(f32[2,48,1024]{2,1,0:T(8,128)} %sci.1, f32[2,48,1024]{2,1,0:T(8,128)} %tiles.1, s32[2,2]{1,0:T(2,128)} %pairs.1, s32[2]{0:T(128)} %offs.1, f32[32,128]{1,0:T(8,128)} %pad.7.brow, f32[32,128]{1,0:T(8,128)} %pad.8.bcol), custom_call_target="tpu_custom_call" | custom-call | flops 8000000000 | bytes 2000000 | tf_op jit(solution)/shard_map/pallas_call | solution.py:447
  112.2 0.0 copy-start
  112.2 1.8 %copy.10 = f32[2,48,1024]{2,1,0:T(8,128)} copy(f32[2,48,1024]{2,1,0:T(8,128)} %get-tuple-element.4) | data formatting | bytes 786432
  114.0 0.0 copy-done
  114.0 0.7 copy.11
Async XLA Ops:
  0.6 1.3 %copy-start.1 = (f32[31,31]{1,0:T(8,128)S(1)}, f32[31,31]{1,0:T(8,128)}, u32[]{:S(2)}) copy-start(f32[31,31]{1,0:T(8,128)} %param.11) | copy-start | bytes 11536
  112.2 1.8 %copy-start = (f32[2,48,1024]{2,1,0:T(8,128)S(1)}, f32[2,48,1024]{2,1,0:T(8,128)}, u32[]{:S(2)}) copy-start(f32[2,48,1024]{2,1,0:T(8,128)} %get-tuple-element.5) | copy-start | bytes 1179652

commit v7 on v3

--- a/solution.py
+++ b/solution.py
@@ -359,16 +359,16 @@
 
     assemble(0)
     relay(1, 1, 0)
+    edges(0)
     relay(1, 1, 1)
-    edges(0)
     row_step()
+    column_step(0)
     relay(1, 1, 2)
-    column_step(0)
     column_step(1)
+    column_step(2)
     relay(2, 1, 0)
-    column_step(2)
+    column_step(3)
     relay(2, 1, 1)
-    column_step(3)
     products(0)
     relay(2, 1, 2)
     solve(0, nothing)

time: 114 us -> 117 us (1.026)
  the two profiles are of different devices: /device:TPU:3 before, /device:TPU:1 now
where the time goes in v7:
time: 117 us; the launch traced here: 116 us
  Pallas kernels  111 us (95%)
  local copies, waits for them, and re-layouts  4.59 us (4%)
    pallas_call x1, Pallas kernels, on_device(): pl.pallas_call(functools.partial(kernel, float(pixels)), out_shape=[jax.S...  111 us
    unnamed x6, local copies, waits for them, and re-layouts  2.57 us

profile of v7, /device:TPU:1, one launch (start us, length us, event | category | flops | bytes accessed | tf_op | source)
XLA Modules:
  0.0 116.3 jit_solution(6520189390365816239)
XLA Ops:
  0.6 0.0 copy-start.1
  0.6 1.3 %pad.7.brow = f32[32,128]{1,0:T(8,128)} pad(f32[31,31]{1,0:T(8,128)} %param.10, f32[]{:T(128)} %constant.2.clone.1), padding=0_1x0_97 | pad | bytes 20232 | tf_op jit(solution)/shard_map/jit(_pad)/pad | solution.py:440
  2.0 0.0 copy-done.1
  2.0 0.1 rev.3
  2.0 0.6 pad.8.bcol
  2.7 111.1 %shard_map.77 = (f32[2,48,1024]{2,1,0:T(8,128)}, f32[2,48,1024]{2,1,0:T(8,128)}) custom-call(f32[2,48,1024]{2,1,0:T(8,128)} %sci.1, f32[2,48,1024]{2,1,0:T(8,128)} %tiles.1, s32[2,2]{1,0:T(2,128)} %pairs.1, s32[2]{0:T(128)} %offs.1, f32[32,128]{1,0:T(8,128)} %pad.7.brow, f32[32,128]{1,0:T(8,128)} %pad.8.bcol), custom_call_target="tpu_custom_call" | custom-call | flops 8000000000 | bytes 2000000 | tf_op jit(solution)/shard_map/pallas_call | solution.py:446
  113.7 0.0 copy-start
  113.7 1.8 %copy.10 = f32[2,48,1024]{2,1,0:T(8,128)} copy(f32[2,48,1024]{2,1,0:T(8,128)} %get-tuple-element.4) | data formatting | bytes 786432
  115.6 0.0 copy-done
  115.6 0.7 copy.11
Async XLA Ops:
  0.6 1.3 %copy-start.1 = (f32[31,31]{1,0:T(8,128)S(1)}, f32[31,31]{1,0:T(8,128)}, u32[]{:S(2)}) copy-start(f32[31,31]{1,0:T(8,128)} %param.11) | copy-start | bytes 11536
  113.7 1.8 %copy-start = (f32[2,48,1024]{2,1,0:T(8,128)S(1)}, f32[2,48,1024]{2,1,0:T(8,128)}, u32[]{:S(2)}) copy-start(f32[2,48,1024]{2,1,0:T(8,128)} %get-tuple-element.5) | copy-start | bytes 1179652
